TPU v7x, 128 devices: a whole 4x4x4 slice. The times are simulated.
128 devices in a mesh: dp: 16 (over z, y), tensor: 8 (over x, core).
Axes of the slice: x: 4, y: 4, z: 4, core: 2. Of those that a mesh axis runs over, the one named last changes fastest.
Arguments:
- hidden_in: bfloat16 [16, 1024, 1024], P('dp', 'tensor'), may hold values from -6 to 6
- first_gain: bfloat16 [1024], replicated, may hold values from 0.5 to 1.5
- first_shift: bfloat16 [1024], replicated, may hold values from -1 to 1
- second_gain: bfloat16 [1024], replicated, may hold values from 0.5 to 1.5
- second_shift: bfloat16 [1024], replicated, may hold values from -1 to 1
- qkv_weight: bfloat16 [3, 1024, 1024], P(None, None, 'tensor'), may hold values from -0.1875 to 0.1875
- qkv_bias: bfloat16 [3, 1024], P(None, 'tensor'), may hold values from -1 to 1
- dense_weight: bfloat16 [1024, 1024], P('tensor'), may hold values from -3 to 3
- up_weight: bfloat16 [1024, 4096], P(None, 'tensor'), may hold values from -0.1875 to 0.1875
- up_bias: bfloat16 [4096], P('tensor'), may hold values from -1 to 1
- down_weight: bfloat16 [4096, 1024], P('tensor'), may hold values from -0.09375 to 0.09375
- out_bias: bfloat16 [1024], replicated, may hold values from -2.5 to 2.5
- segments: int32 [16, 1024], P('dp'), may hold values from 0 to 2, as said below
- positions: int32 [16, 1024], P('dp'), may hold values from 0 to 1023, as said below
- cotangent: bfloat16 [16, 1024, 1024], P('dp', 'tensor'), may hold values from -6 to 6
Outputs:
- activations: bfloat16 [16, 1024, 1024], P('dp', 'tensor')
- input_grad: float32 [16, 1024, 1024], P('dp', 'tensor')
- qkv_weight_grad: float32 [3, 1024, 1024], P(None, None, 'tensor')
- qkv_bias_grad: float32 [3, 1024], P(None, 'tensor')
- dense_weight_grad: float32 [1024, 1024], P('tensor')
- up_weight_grad: float32 [1024, 4096], P(None, 'tensor')
- up_bias_grad: float32 [4096], P('tensor')
- down_weight_grad: float32 [4096, 1024], P('tensor')
- out_bias_grad: float32 [1024], replicated
- first_gain_grad: float32 [1024], replicated
- first_shift_grad: float32 [1024], replicated
- second_gain_grad: float32 [1024], replicated
- second_shift_grad: float32 [1024], replicated
Inputs may be any that keep to these rules, and one draw needn't show every extreme that they name: Segment numbers never fall along a sequence, and every sequence holds segments 0, 1 and 2. `positions`: within a segment the position rises by one from token to token; segments 1 and 2 start at 0, and segment 0 ends at 1023.
All inputs are finite; a program needn't handle non-finite values.
Results may differ from a plain program's by a relative error of at most 0.012.
Values may be sent and summed in bfloat16 or wider, within the bound.
A program may use at most 128 MiB of HBM per device.

v0:
```python
import jax
import jax.numpy as jnp
from jax import lax
from jax.sharding import PartitionSpec as P

D = 1024
HEADS = 16
HEAD_DIM = 64
ROT = 16
SEQ = 1024


norm_epsilon = 1e-05


def layer_norm(values, norm_gain, norm_shift):
    mean_value = jnp.mean(values, axis=-1, keepdims=True)
    centered = values - mean_value
    spread = jnp.mean(centered * centered, axis=-1, keepdims=True)
    return centered * lax.rsqrt(spread + norm_epsilon) * norm_gain + norm_shift


def both_norms(values, gain_one, shift_one, gain_two, shift_two):
    return (layer_norm(values, gain_one, shift_one), layer_norm(values, gain_two, shift_two))


def exact_gelu(values):
    return jax.nn.gelu(values, approximate=False)


def angles(positions):
    half_rot = ROT // 2
    frequency = 10000.0 ** (-2.0 * jnp.arange(half_rot, dtype=jnp.float32) / ROT)
    phase_angle = positions.astype(jnp.float32)[..., None] * frequency
    return (jnp.cos(phase_angle), jnp.sin(phase_angle))


def rotate(values, cos_table, sine_table):
    half_rot = cos_table.shape[-1]
    first_half = values[..., :half_rot]
    second_half = values[..., half_rot : 2 * half_rot]
    cos_heads = cos_table[..., None, :]
    sin_heads = sine_table[..., None, :]
    return jnp.concatenate(
        [
            first_half * cos_heads - second_half * sin_heads,
            second_half * cos_heads + first_half * sin_heads,
            values[..., 2 * half_rot :],
        ],
        axis=-1,
    )


def allowed_keys(segment_row, first_query, query_count):
    query_place = first_query + jnp.arange(query_count, dtype=jnp.int32)
    key_place = jnp.arange(segment_row.shape[0], dtype=jnp.int32)
    query_segment = lax.dynamic_slice_in_dim(segment_row, first_query, query_count, 0)
    return (key_place[None, :] <= query_place[:, None]) & (
        segment_row[None, :] == query_segment[:, None]
    )


def local(
    hidden_in,
    first_gain,
    first_shift,
    second_gain,
    second_shift,
    qkv_weight,
    qkv_bias,
    dense_weight,
    up_weight,
    up_bias,
    down_weight,
    out_bias,
    segments,
    positions,
    cotangent,
):
    tensor_size = lax.axis_size("tensor")
    seq_count = hidden_in.shape[0]
    local_heads = HEADS // tensor_size
    local_width = local_heads * HEAD_DIM
    row_total = seq_count * SEQ
    block_rows = min(512, SEQ)
    block_count = SEQ // block_rows
    head_scale = HEAD_DIM ** (-0.5)
    head_shape = (row_total, local_heads, HEAD_DIM)
    seq_shape = (seq_count, SEQ, local_heads, HEAD_DIM)
    own_rows = hidden_in.astype(jnp.float32)
    gain_one_full = first_gain.astype(jnp.float32)
    gain_two_full = second_gain.astype(jnp.float32)
    (normed_one, normed_two), norms_back = jax.vjp(
        both_norms,
        own_rows,
        gain_one_full,
        first_shift.astype(jnp.float32),
        gain_two_full,
        second_shift.astype(jnp.float32),
    )
    low_one = normed_one.astype(jnp.bfloat16)
    low_two = normed_two.astype(jnp.bfloat16)
    full_one, full_two = (
        lax.all_gather(low_one, "tensor", axis=1, tiled=True),
        lax.all_gather(low_two, "tensor", axis=1, tiled=True),
    )
    flat_one = full_one.reshape(row_total, D)
    flat_two = full_two.reshape(row_total, D)
    cos_table, sine_table = angles(positions.reshape(row_total))
    projected = jnp.einsum("rd,idc->irc", flat_one, qkv_weight, preferred_element_type=jnp.float32)
    projected = projected + qkv_bias.astype(jnp.float32)[:, None, :]
    query_pre = projected[0].reshape(head_shape)
    key_pre = projected[1].reshape(head_shape)
    value_pre = projected[2].reshape(head_shape)

    def turn_query(values):
        return rotate(values, cos_table, sine_table) * head_scale

    def turn_key(values):
        return rotate(values, cos_table, sine_table)

    query_turned, query_back = jax.vjp(turn_query, query_pre)
    key_turned, key_back = jax.vjp(turn_key, key_pre)
    query_low = query_turned.astype(jnp.bfloat16).reshape(seq_shape)
    key_low = key_turned.astype(jnp.bfloat16).reshape(seq_shape)
    value_low = value_pre.astype(jnp.bfloat16).reshape(seq_shape)

    def forward_sequence(operands):
        query_seq, key_seq, value_seq, segment_row = operands

        def forward_block(block_index):
            first_query = block_index * block_rows
            query_block = lax.dynamic_slice_in_dim(query_seq, first_query, block_rows, 0)
            allowed = allowed_keys(segment_row, first_query, block_rows)
            scores = jnp.einsum(
                "qhd,khd->hqk", query_block, key_seq, preferred_element_type=jnp.float32
            )
            scores = jnp.where(allowed[None], scores, -1e30)
            row_peak = jnp.max(scores, axis=-1, keepdims=True)
            exp_scores = jnp.exp(scores - row_peak)
            totals = jnp.sum(exp_scores, axis=-1, keepdims=True)
            soft_weights = (exp_scores / totals).astype(jnp.bfloat16)
            mixed_block = jnp.einsum(
                "hqk,khd->qhd", soft_weights, value_seq, preferred_element_type=jnp.float32
            )
            return (mixed_block, (row_peak + jnp.log(totals))[..., 0])

        mixed_blocks, log_blocks = lax.map(forward_block, jnp.arange(block_count, dtype=jnp.int32))
        return (mixed_blocks.reshape(SEQ, local_heads, HEAD_DIM), log_blocks)

    attended, log_totals = lax.map(forward_sequence, (query_low, key_low, value_low, segments))
    mixed_low = attended.reshape(row_total, local_width).astype(jnp.bfloat16)
    gate_in = jnp.dot(flat_two, up_weight, preferred_element_type=jnp.float32) + up_bias.astype(
        jnp.float32
    )
    active, gelu_back = jax.vjp(exact_gelu, gate_in)
    active_low = active.astype(jnp.bfloat16)
    partial_out = jnp.dot(mixed_low, dense_weight, preferred_element_type=jnp.float32)
    partial_out = partial_out + jnp.dot(active_low, down_weight, preferred_element_type=jnp.float32)
    summed = lax.psum_scatter(
        partial_out.reshape(seq_count, SEQ, D), "tensor", scatter_dimension=1, tiled=True
    )
    activations = (own_rows + summed + out_bias.astype(jnp.float32)).astype(jnp.bfloat16)
    grad_full = lax.all_gather(cotangent, "tensor", axis=1, tiled=True)
    grad_rows = grad_full.reshape(row_total, D)
    grad_down = jnp.einsum("rf,rd->fd", active_low, grad_rows, preferred_element_type=jnp.float32)
    grad_active = jnp.einsum(
        "rd,fd->rf", grad_rows, down_weight, preferred_element_type=jnp.float32
    )
    grad_gate = gelu_back(grad_active)[0].astype(jnp.bfloat16)
    grad_up = jnp.einsum("rd,rf->df", flat_two, grad_gate, preferred_element_type=jnp.float32)
    grad_up_bias = jnp.sum(grad_gate.astype(jnp.float32), axis=0)
    grad_norm_two = jnp.einsum(
        "rf,df->rd", grad_gate, up_weight, preferred_element_type=jnp.float32
    )
    grad_dense = jnp.einsum("rc,rd->cd", mixed_low, grad_rows, preferred_element_type=jnp.float32)
    grad_mixed = jnp.einsum(
        "rd,cd->rc", grad_rows, dense_weight, preferred_element_type=jnp.float32
    )
    grad_mixed = grad_mixed.astype(jnp.bfloat16).reshape(seq_shape)

    def backward_sequence(operands):
        query_seq, key_seq, value_seq, segment_row, grad_seq, log_seq = operands

        def backward_block(carried, block_index):
            grad_keys, grad_values = carried
            first_query = block_index * block_rows
            query_block = lax.dynamic_slice_in_dim(query_seq, first_query, block_rows, 0)
            grad_block = lax.dynamic_slice_in_dim(grad_seq, first_query, block_rows, 0)
            log_block = lax.dynamic_index_in_dim(log_seq, block_index, 0, keepdims=False)
            allowed = allowed_keys(segment_row, first_query, block_rows)
            scores = jnp.einsum(
                "qhd,khd->hqk", query_block, key_seq, preferred_element_type=jnp.float32
            )
            soft_weights = jnp.where(allowed[None], jnp.exp(scores - log_block[..., None]), 0.0)
            grad_values = grad_values + jnp.einsum(
                "hqk,qhd->khd",
                soft_weights.astype(jnp.bfloat16),
                grad_block,
                preferred_element_type=jnp.float32,
            )
            grad_weights = jnp.einsum(
                "qhd,khd->hqk", grad_block, value_seq, preferred_element_type=jnp.float32
            )
            centre = jnp.sum(soft_weights * grad_weights, axis=-1, keepdims=True)
            grad_scores = (soft_weights * (grad_weights - centre)).astype(jnp.bfloat16)
            grad_query = jnp.einsum(
                "hqk,khd->qhd", grad_scores, key_seq, preferred_element_type=jnp.float32
            )
            grad_keys = grad_keys + jnp.einsum(
                "hqk,qhd->khd", grad_scores, query_block, preferred_element_type=jnp.float32
            )
            return ((grad_keys, grad_values), grad_query)

        zero_state = jnp.zeros((SEQ, local_heads, HEAD_DIM), jnp.float32)
        (grad_keys, grad_values), grad_queries = lax.scan(
            backward_block, (zero_state, zero_state), jnp.arange(block_count, dtype=jnp.int32)
        )
        return (grad_queries.reshape(SEQ, local_heads, HEAD_DIM), grad_keys, grad_values)

    grad_query_all, grad_key_all, grad_value_all = lax.map(
        backward_sequence, (query_low, key_low, value_low, segments, grad_mixed, log_totals)
    )
    grad_query_pre = query_back(grad_query_all.reshape(head_shape))[0].astype(jnp.bfloat16)
    grad_key_pre = key_back(grad_key_all.reshape(head_shape))[0].astype(jnp.bfloat16)
    grad_value_pre = grad_value_all.reshape(head_shape).astype(jnp.bfloat16)
    grad_projected = jnp.stack([grad_query_pre, grad_key_pre, grad_value_pre]).reshape(
        3, row_total, local_width
    )
    grad_qkv = jnp.einsum(
        "rd,irc->idc", flat_one, grad_projected, preferred_element_type=jnp.float32
    )
    grad_qkv_bias = jnp.sum(grad_projected.astype(jnp.float32), axis=1)
    grad_norm_one = jnp.einsum(
        "irc,idc->rd", grad_projected, qkv_weight, preferred_element_type=jnp.float32
    )
    grad_qkv, grad_qkv_bias, grad_dense, grad_up, grad_up_bias, grad_down = lax.psum(
        (grad_qkv, grad_qkv_bias, grad_dense, grad_up, grad_up_bias, grad_down), "dp"
    )
    cotangent_rows = cotangent.astype(jnp.float32)
    grad_one, grad_two = (
        lax.psum_scatter(
            grad_norm_one.reshape(seq_count, SEQ, D), "tensor", scatter_dimension=1, tiled=True
        ),
        lax.psum_scatter(
            grad_norm_two.reshape(seq_count, SEQ, D), "tensor", scatter_dimension=1, tiled=True
        ),
    )
    grad_in_rows, grad_gain_one, grad_shift_one, grad_gain_two, grad_shift_two = norms_back(
        (grad_one, grad_two)
    )
    input_grad = cotangent_rows + grad_in_rows
    grad_out_bias = jnp.sum(cotangent_rows, axis=(0, 1))
    grad_gain_one, grad_shift_one, grad_gain_two, grad_shift_two, grad_out_bias = lax.psum(
        (grad_gain_one, grad_shift_one, grad_gain_two, grad_shift_two, grad_out_bias),
        ("dp", "tensor"),
    )
    return (
        activations,
        input_grad,
        grad_qkv,
        grad_qkv_bias,
        grad_dense,
        grad_up,
        grad_up_bias,
        grad_down,
        grad_out_bias,
        grad_gain_one,
        grad_shift_one,
        grad_gain_two,
        grad_shift_two,
    )


def solution(mesh):
    placed = (
        P("dp", "tensor", None),
        P(),
        P(),
        P(),
        P(),
        P(None, None, "tensor"),
        P(None, "tensor"),
        P("tensor", None),
        P(None, "tensor"),
        P("tensor"),
        P("tensor", None),
        P(),
        P("dp", None),
        P("dp", None),
        P("dp", "tensor", None),
    )
    return jax.shard_map(
        local,
        mesh=mesh,
        in_specs=placed,
        out_specs=(
            P("dp", "tensor", None),
            P("dp", "tensor", None),
            P(None, None, "tensor"),
            P(None, "tensor"),
            P("tensor", None),
            P(None, "tensor"),
            P("tensor"),
            P("tensor", None),
            P(),
            P(),
            P(),
            P(),
            P(),
        ),
        check_vma=False,
    )
```

profile of v0, /device:TPU:0, one launch (start us, length us, event | category | flops | bytes accessed | tf_op | source)
XLA Modules:
  0.0 445.9 jit_solution(4316070711077627079)
XLA Ops:
  7.3 1.2 convert_reduce_fusion.2
  8.5 1.2 fusion.81
  12.4 2.0 fusion.78
  16.2 1.2 copy.34
  17.5 24.7 %all-gather.4.cloned.1.call-done = bf16[1,1024,1024]{2,1,0:T(8,128)(2,1)} async-done(((bf16[1,128,1024]{2,1,0:T(8,128)(2,1)}), bf16[1,1024,1024]{2,1,0:T(8,128)(2,1)}) %all-gather.4.cloned.1.call-update) | async-done | bytes 2097168 | tf_op jit(solution)/shard_map/all_gather | solution.py:104
  42.2 2.8 fusion.50
  45.9 10.8 %while.49 = (s32[]{:T(128)}, bf16[2,512,2,64]{1,3,2,0:T(8,128)(2,1)S(1)}, f32[2,2,512]{2,1,0:T(2,128)S(1)}, s32[2]{0:T(128)S(1)}, s32[1024]{0:T(1024)S(1)}, /*in...) while((s32[]{:T(128)}, ...), condition=%wide.region_5.6_spmd.clone, body=%wide.region_2.5_spmd.sunk.clone | while | flops 279444992 | bytes 15644851 | solution.py:148
  48.7 1.1 fusion.157
  49.8 1.4 fusion.158
  55.2 1.4 fusion.158
  57.4 12.0 %all-gather.8.cloned.1.call-done = bf16[1,1024,1024]{2,1,0:T(8,128)(2,1)} async-done(((bf16[1,128,1024]{2,1,0:T(8,128)(2,1)}), bf16[1,1024,1024]{2,1,0:T(8,128)(2,1)}) %all-gather.8.cloned.1.call-update) | async-done | bytes 2097168 | tf_op jit(solution)/shard_map/all_gather | solution.py:164
  69.4 2.4 fusion.62
  71.8 22.6 %while.50 = (s32[]{:T(128)}, f32[1024,2,64]{0,2,1:T(8,128)S(1)}, f32[1024,2,64]{0,2,1:T(8,128)S(1)}, f32[2,512,2,64]{1,3,2,0:T(8,128)}, s32[2]{0:T(128)S(1)}, /*...) while((s32[]{:T(128)}, f32[1024,2,64]{0,2,1:T(8,128)S(1)}, ...), condition=%wide.region_12.13_spmd.clone.clone, body=%wide.region_10.12_spmd.clone.sunk.clone | while | flops 685768192 | bytes 41462064 | solution.py:216
  76.4 1.2 fusion.171
  77.6 1.7 multiply_reduce_fusion.3
  79.3 1.2 multiply_convert_fusion.4
  87.7 1.2 fusion.171
  88.9 1.7 multiply_reduce_fusion.3
  90.6 1.2 multiply_convert_fusion.4
  94.5 1.3 multiply_bitcast_fusion
  96.8 1.3 copy.38
  98.0 1.8 copy.37
  99.8 1.8 convert_element_type.128
  101.6 1.8 copy.39
  103.4 1.2 copy.35
  105.4 1.2 fusion.40
  106.6 7.3 %multiply_convert_fusion.1 = (bf16[1024,512]{1,0:T(8,128)(2,1)S(1)}, f32[1024,512]{1,0:T(8,128)S(1)}, f32[1024,512]{1,0:T(8,128)S(1)}) fusion(f32[512]{0:T(512)S(1)} %convert_element_type.119, bf16[1024,512]{1,0:T(8,128)(2,1)S(1)} %copy-done, bf16[1,1024,1024]{2,1,0:T(8,128)(2,1)} %all-gather.6.cloned.1.call-done), kind=kOutput, calls=%fused_computation.67 | convolution fusion | flops 1108344832 | bytes 8390656 | tf_op jit(solution)/shard_map/dot_general | solution.py:153
  113.9 2.6 fusion.38
  116.5 2.0 convert_reduce_fusion
  118.6 2.6 fusion.46
  121.2 2.2 fusion.57
  123.4 1.1 copy-done.9
  124.5 3.2 convolution_bitcast_fusion.2
  127.8 1.1 copy-done.42
  129.0 3.3 convolution_bitcast_fusion.3
  134.8 3.2 add_bitcast_fusion
  138.8 42.2 %all-reduce.7 = (f32[3,128]{1,0:T(4,128)}, f32[512]{0:T(512)}) all-reduce(f32[3,128]{1,0:T(4,128)S(1)} %convert_reduce_fusion.1, f32[512]{0:T(512)S(1)} %get-tuple-element.324), channel_id=1, replica_groups=mesh['dp'=16,'tensor'=8] {'dp'}, use_global_device_ids=true, to_apply=%region_18.19 | all-reduce | flops 896 | bytes 7168 | tf_op jit(solution)/shard_map/psum | solution.py:237
  181.1 66.1 %all-reduce.11.cloned.1.call-done = (f32[3,1024,128]{1,2,0:T(8,128)}, f32[128,1024]{1,0:T(8,128)}, f32[1024,512]{1,0:T(8,128)}, f32[512,1024]{1,0:T(8,128)}) async-done(((f32[3,1024,128]{1,2,0:T(8,128)}, f32[128,1024]{1,0:T(8,128)}, f32[1024,512]{1,0:T(8,128)}, f32[512,1024]{1,0:T(8,128)}), (f32[3,1024,128]{1,2,0:T(8,128)}, f32[128,1024]{1,0:T(8,128)}, f32[1024,512]{1,0:T(8,128)}, ...) | async-done | bytes 6291472 | tf_op jit(solution)/shard_map/psum | solution.py:237
  247.2 3.0 copy.41
  250.2 36.9 %reduce-scatter.8.cloned.1.call-done = f32[1,128,1024]{2,1,0:T(8,128)} async-done(((f32[1,1024,1024]{2,1,0:T(8,128)}), f32[1,128,1024]{2,1,0:T(8,128)}) %reduce-scatter.8.cloned.1.call-update) | async-done | bytes 524304 | tf_op jit(solution)/shard_map/reduce_scatter | solution.py:242
  287.1 39.3 %reduce-scatter.6.cloned.1.call-done = f32[1,128,1024]{2,1,0:T(8,128)} async-done(((f32[1,1024,1024]{2,1,0:T(8,128)}), f32[1,128,1024]{2,1,0:T(8,128)}) %reduce-scatter.6.cloned.1.call-update) | async-done | bytes 524304 | tf_op jit(solution)/shard_map/reduce_scatter | solution.py:245
  326.4 1.6 fusion.91
  328.0 1.7 fusion.80
  329.8 36.0 %reduce-scatter.4.cloned.1.call-done = f32[1,128,1024]{2,1,0:T(8,128)} async-done(((f32[1,1024,1024]{2,1,0:T(8,128)}), f32[1,128,1024]{2,1,0:T(8,128)}) %reduce-scatter.4.cloned.1.call-update) | async-done | bytes 524304 | tf_op jit(solution)/shard_map/reduce_scatter | solution.py:160
  365.8 2.3 convert_reduce_fusion.3
  368.0 65.7 %all-reduce.6 = (f32[1024]{0:T(1024)}, f32[1024]{0:T(1024)}, f32[1024]{0:T(1024)}, f32[1024]{0:T(1024)}, f32[1024]{0:T(1024)}) all-reduce(f32[1024]{0:T(1024)S(1)} %get-tuple-element.314, f32[1024]{0:T(1024)S(1)} %get-tuple-element.242, f32[1024]{0:T(1024)S(1)} %get-tuple-element.239, ...), channel_id=1, replica_groups=mesh['dp'=16,'tensor'=8] {'dp','tensor'}, use_global_device_ids=true, to_apply=%region_25.26 | all-reduce | flops 5120 | bytes 40960 | tf_op jit(solution)/shard_map/psum | solution.py:254
  434.5 3.2 copy.76
  437.8 1.3 copy.77
  (172 shorter events, 26.7 us)
Async XLA Ops:
  7.2 99.5 %copy-start = (bf16[1024,512]{1,0:T(8,128)(2,1)S(1)}, bf16[1024,512]{1,0:T(8,128)(2,1)}, u32[]{:S(2)}) copy-start(bf16[1024,512]{1,0:T(8,128)(2,1)} %param.27) | copy-start | bytes 3145732
  7.2 8.9 %copy-start.37 = (bf16[512]{0:T(512)(128)(2,1)S(1)}, bf16[512]{0:T(512)(128)(2,1)}, u32[]{:S(2)}) copy-start(bf16[512]{0:T(512)(128)(2,1)} %param.28) | copy-start | bytes 3076
  7.2 8.9 %copy-start.38 = (bf16[3,128]{1,0:T(4,128)(2,1)S(1)}, bf16[3,128]{1,0:T(4,128)(2,1)}, u32[]{:S(2)}) copy-start(bf16[3,128]{1,0:T(4,128)(2,1)} %param.25) | copy-start | bytes 2308
  7.2 8.9 %copy-start.33 = (s32[1,1024]{1,0:T(1,128)S(1)}, s32[1,1024]{1,0:T(1,128)}, u32[]{:S(2)}) copy-start(s32[1,1024]{1,0:T(1,128)} %param.32) | copy-start | bytes 12292
  7.2 8.9 %copy-start.8 = (bf16[3,1024,128]{2,1,0:T(8,128)(2,1)S(1)}, bf16[3,1024,128]{2,1,0:T(8,128)(2,1)}, u32[]{:S(2)}) copy-start(bf16[3,1024,128]{2,1,0:T(8,128)(2,1)} %param.24) | copy-start | bytes 2359300
  7.2 35.0 %all-gather.4.cloned.1.call-start = ((), (), s32[]{:S(2)}) async-start(), calls=%async_computation.3 | async-start | bytes 2359296 | tf_op jit(solution)/shard_map/all_gather | solution.py:104
  8.5 6.0 %copy-start.29 = (f32[128]{0:T(128)}, f32[128]{0:T(128)S(1)}, u32[]{:S(2)}) copy-start(f32[128]{0:T(128)S(1)} %broadcast_multiply_fusion) | copy-start | bytes 1540
  9.7 6.4 %copy-start.34 = (f32[128]{0:T(128)}, f32[128]{0:T(128)S(1)}, u32[]{:S(2)}) copy-start(f32[128]{0:T(128)S(1)} %fusion.81) | copy-start | bytes 1540
  9.7 4.8 %copy-start.31 = (f32[128]{0:T(128)}, f32[128]{0:T(128)S(1)}, u32[]{:S(2)}) copy-start(f32[128]{0:T(128)S(1)} %fusion.87) | copy-start | bytes 1540
  10.4 2.1 copy-start.25
  11.1 3.4 copy-start.27
  14.5 54.9 %all-gather.8.cloned.1.call-start = ((), (), s32[]{:S(2)}) async-start(), calls=%async_computation.6 | async-start | bytes 2359296 | tf_op jit(solution)/shard_map/all_gather | solution.py:164
  15.2 91.4 %all-gather.6.cloned.1.call-start = ((), (), s32[]{:S(2)}) async-start(), calls=%async_computation.4 | async-start | bytes 2359296 | tf_op jit(solution)/shard_map/all_gather | solution.py:105
  16.0 231.2 %all-reduce.11.cloned.1.call-start = ((), (), s32[]{:S(2)}) async-start(), calls=%async_computation.9 | async-start | bytes 12582912 | tf_op jit(solution)/shard_map/psum | solution.py:237
  45.9 23.5 %copy-start.17 = (bf16[128,1024]{1,0:T(8,128)(2,1)S(1)}, bf16[128,1024]{1,0:T(8,128)(2,1)}, u32[]{:S(2)}) copy-start(bf16[128,1024]{1,0:T(8,128)(2,1)} %param.26) | copy-start | bytes 786436
  80.5 1.1 copy-start.23
  82.4 0.8 copy-start.24
  91.8 1.0 copy-start.23
  93.7 0.8 copy-start.24
  94.5 1.4 copy-start.2
  96.8 8.6 %copy-start.1 = (bf16[1,1024,1024]{2,1,0:T(8,128)(2,1)S(1)}, bf16[1,1024,1024]{2,1,0:T(8,128)(2,1)}, u32[]{:S(2)}) copy-start(bf16[1,1024,1024]{2,1,0:T(8,128)(2,1)} %all-gather.8.cloned.1.call-done) | copy-start | bytes 6291460
  113.9 2.6 copy-start.4
  113.9 2.6 copy-start.15
  116.5 2.0 copy-start.40
  118.6 2.7 copy-start.41
  118.6 2.6 copy-start.10
  118.6 2.6 copy-start.11
  118.6 2.6 copy-start.39
  123.4 1.1 copy-start.9
  123.4 163.7 %reduce-scatter.8.cloned.1.call-start = ((), (), s32[]{:S(2)}) async-start(), calls=%async_computation.8 | async-start | bytes 4718592 | tf_op jit(solution)/shard_map/reduce_scatter | solution.py:242
  127.7 1.2 copy-start.42
  127.8 198.6 %reduce-scatter.6.cloned.1.call-start = ((), (), s32[]{:S(2)}) async-start(), calls=%async_computation.7 | async-start | bytes 4718592 | tf_op jit(solution)/shard_map/reduce_scatter | solution.py:245
  132.2 1.0 copy-start.13
  132.2 1.2 copy-start.18
  132.3 1.9 copy-start.5
  132.3 233.5 %reduce-scatter.4.cloned.1.call-start = ((), (), s32[]{:S(2)}) async-start(), calls=%async_computation.5 | async-start | bytes 4718592 | tf_op jit(solution)/shard_map/reduce_scatter | solution.py:160
  133.4 1.3 copy-start.16
  138.7 187.7 %copy-start.3 = (bf16[1,128,1024]{2,1,0:T(8,128)(2,1)S(1)}, bf16[1,128,1024]{2,1,0:T(8,128)(2,1)}, u32[]{:S(2)}) copy-start(bf16[1,128,1024]{2,1,0:T(8,128)(2,1)} %param.19) | copy-start | bytes 786436
  138.7 187.7 %copy-start.26 = (f32[1024]{0:T(1024)S(1)}, f32[1024]{0:T(1024)}, u32[]{:S(2)}) copy-start(f32[1024]{0:T(1024)} %copy-done.25) | copy-start | bytes 12292
  138.7 187.7 %copy-start.28 = (f32[1024]{0:T(1024)S(1)}, f32[1024]{0:T(1024)}, u32[]{:S(2)}) copy-start(f32[1024]{0:T(1024)} %copy-done.27) | copy-start | bytes 12292
  138.7 187.7 %copy-start.30 = (f32[128]{0:T(128)S(1)}, f32[128]{0:T(128)}, u32[]{:S(2)}) copy-start(f32[128]{0:T(128)} %copy-done.29) | copy-start | bytes 1540
  247.2 80.8 %copy-start.35 = (f32[128]{0:T(128)S(1)}, f32[128]{0:T(128)}, u32[]{:S(2)}) copy-start(f32[128]{0:T(128)} %copy-done.34) | copy-start | bytes 1540
  247.2 80.8 %copy-start.32 = (f32[128]{0:T(128)S(1)}, f32[128]{0:T(128)}, u32[]{:S(2)}) copy-start(f32[128]{0:T(128)} %copy-done.31) | copy-start | bytes 1540
  250.2 115.5 %copy-start.19 = (bf16[1,128,1024]{2,1,0:T(8,128)(2,1)S(1)}, bf16[1,128,1024]{2,1,0:T(8,128)(2,1)}, u32[]{:S(2)}) copy-start(bf16[1,128,1024]{2,1,0:T(8,128)(2,1)} %param.33) | copy-start | bytes 786436
  287.1 78.7 %copy-start.6 = (f32[1,128,1024]{2,1,0:T(8,128)S(1)}, f32[1,128,1024]{2,1,0:T(8,128)}, u32[]{:S(2)}) copy-start(f32[1,128,1024]{2,1,0:T(8,128)} %reduce-scatter.8.cloned.1.call-done) | copy-start | bytes 1572868
  326.4 39.4 %copy-start.7 = (f32[1,128,1024]{2,1,0:T(8,128)S(1)}, f32[1,128,1024]{2,1,0:T(8,128)}, u32[]{:S(2)}) copy-start(f32[1,128,1024]{2,1,0:T(8,128)} %reduce-scatter.6.cloned.1.call-done) | copy-start | bytes 1572868
  328.0 105.7 %copy-start.22 = (f32[128,1024]{1,0:T(8,128)S(1)}, f32[128,1024]{1,0:T(8,128)}, u32[]{:S(2)}) copy-start(f32[128,1024]{1,0:T(8,128)} %get-tuple-element.571) | copy-start | bytes 1572868
  434.5 3.2 copy-start.14
  (4 other events, 2.8 us)
Sparse Core Ops, SparseCore 0:
  14.6 27.5 all-gather.3
  43.9 25.4 all-gather.7
  71.7 25.4 all-gather.5
  123.5 123.6 all-reduce.10
  249.6 37.4 reduce-scatter.7
  289.5 36.8 reduce-scatter.5
  328.9 36.8 reduce-scatter.3
where the time goes:
time: 448 us; the launch traced here: 446 us
  waiting for transfers between devices  216 us (48%)
  blocking collectives  108 us (24%)
  matrix products  48.3 us (11%)
  local copies, waits for them, and re-layouts  27.6 us (6%)
  other arithmetic  24 us (5%)
  between operations  14.7 us (3%)
  loops' own time  6.69 us (1%)
    psum x1, waiting for transfers between devices, local(): lax.psum((grad_qkv, grad_qkv_bias, grad_dense, grad_up, grad_up_bias, gra...  66.1 us
    psum x1, blocking collectives, local(): lax.psum((grad_gain_one, grad_shift_one, grad_gain_two, grad_shift_two, g...  65.7 us
    psum x1, blocking collectives, local(): lax.psum((grad_qkv, grad_qkv_bias, grad_dense, grad_up, grad_up_bias, gra...  42.2 us
    reduce_scatter x1, waiting for transfers between devices, local(): lax.psum_scatter(grad_norm_two.reshape(seq_count, SEQ, D), 'tensor', scat...  39.3 us
    reduce_scatter x1, waiting for transfers between devices, local(): lax.psum_scatter(grad_norm_one.reshape(seq_count, SEQ, D), 'tensor', scat...  36.9 us
    reduce_scatter x1, waiting for transfers between devices, local(): lax.psum_scatter(partial_out.reshape(seq_count, SEQ, D), 'tensor', scatte...  36 us
    all_gather x1, waiting for transfers between devices, local(): lax.all_gather(low_one, 'tensor', axis=1, tiled=True)  24.7 us
    unnamed x88, local copies, waits for them, and re-layouts  16.1 us
  transfers between devices with their start and end apart: 7, of which 6 were waited for; matrix products, arithmetic and copies ran while one was open for 13% of the time, Pallas kernels for 0%

commit v1 on v0

v1 whole, which is shorter than its diff:
```python
import jax
import jax.numpy as jnp
from jax import lax
from jax.experimental import pallas as pl
from jax.experimental.pallas import tpu as pltpu
from jax.sharding import PartitionSpec as P

D = 1024
HD = 64
SEQ = 1024
F = 512
C = 128
EPS = 1e-05
f32 = jnp.float32
bf16 = jnp.bfloat16
NSEM = 128

YZ = ("yu", "yw", "zu", "zw")
ORD = tuple(tuple(YZ[(q + s) % 4] for s in range(4)) for q in range(4))

SEM_GH = 0
SEM_GC = 12
SEM_RA = 24
SEM_RD = 34
SEM_F = 44
SEM_W = 76
SEM_S = 108


def dot(a, b):
    return lax.dot_general(a, b, (((1,), (0,)), ((), ())), preferred_element_type=f32)


def dot_nt(a, b):
    return lax.dot_general(a, b, (((1,), (1,)), ((), ())), preferred_element_type=f32)


def dot_tn(a, b):
    return lax.dot_general(a, b, (((0,), (0,)), ((), ())), preferred_element_type=f32)


def kernel_body(
    hid_ref, cot_ref, seg_ref, pos_ref, prm_ref, wqkv_ref, wd_ref, wup_ref, wdn_ref,
    act_out, ing_out, of_out, ow_out, sm_out,
    hidf, cotf, xh, n1, n2, act_s, gel, gg, qs, ks, vs, ga, vT, kT, attT, att, gp,
    dk, dv, wcat, wcatT, wupT, wdnT, wdT, ct, st, segc, po, dxh,
    gf, rf, gw, rw, sa, ra, ssa, r1a, r2a, sd, rd, ssd, r1d, r2d, smv, smr,
    ssem, rsem,
):
    dp = lax.axis_index("dp")
    tn = lax.axis_index("tensor")
    c = tn % 2
    x = tn // 2
    y = dp % 4
    z = dp // 4

    def flip(v):
        return v + 1 - 2 * (v % 2)

    def ub(v):
        return (v + v // 2) % 2

    def wb(v):
        return v // 2

    peer = {
        "c": (dp, x * 2 + 1 - c),
        "xu": (dp, flip(x) * 2 + c),
        "xw": (dp, (3 - x) * 2 + c),
        "yu": (z * 4 + flip(y), tn),
        "yw": (z * 4 + 3 - y, tn),
        "zu": (flip(z) * 4 + y, tn),
        "zw": ((3 - z) * 4 + y, tn),
    }
    bit = {"yu": ub(y), "yw": wb(y), "zu": ub(z), "zw": wb(z)}
    xu, xw = ub(x), wb(x)

    pending = []

    def send(i, src, dst, who):
        cp = pltpu.make_async_remote_copy(
            src_ref=src, dst_ref=dst, send_sem=ssem.at[i], recv_sem=rsem.at[i],
            device_id=peer[who], device_id_type=pl.DeviceIdType.MESH,
        )
        cp.start()
        pending.append(cp)
        return cp

    barrier = pltpu.get_barrier_semaphore()
    for who in peer:
        pl.semaphore_signal(barrier, inc=1, device_id=peer[who], device_id_type=pl.DeviceIdType.MESH)
    pl.semaphore_wait(barrier, len(peer))

    own = pl.multiple_of(tn * 128, 128)
    tu = pl.multiple_of((flip(x) * 2 + c) * 128, 128)
    tw = pl.multiple_of(((3 - x) * 2 + c) * 128, 128)
    x2 = flip(3 - x)
    tuw = pl.multiple_of((x2 * 2 + c) * 128, 128)

    class Gather:
        def __init__(self, src, full, base):
            self.src, self.full, self.b, self.cp = src, full, base, {}

        def go(self, i, src, dst, who):
            self.cp[i] = send(self.b + i, src, dst, who)

        def fwd(self, i, row, n, who):
            ref = self.full.at[pl.ds(row, n)]
            self.go(i, ref, ref, who)

        def start(self):
            lo, hi = self.src.at[0, pl.ds(0, 64)], self.src.at[0, pl.ds(64, 64)]
            dlo, dhi = self.full.at[pl.ds(own, 64)], self.full.at[pl.ds(own + 64, 64)]
            self.go(1, lo, dlo, "xu")
            self.go(2, hi, dhi, "xw")
            self.go(3, hi, dhi, "xu")
            self.go(4, lo, dlo, "xw")
            self.go(0, self.src.at[0], self.full.at[pl.ds(own, 128)], "c")
            self.full[pl.ds(own, 128), :] = self.src[0]

        def mid(self):
            self.cp[1].wait_recv()
            self.fwd(5, tu, 64, "xw")
            self.cp[2].wait_recv()
            self.fwd(6, tw + 64, 64, "xu")

        def d2d(self):
            self.cp[3].wait_recv()
            self.fwd(7, tu, 128, "c")
            self.cp[4].wait_recv()
            self.fwd(8, tw, 128, "c")

        def last(self):
            self.cp[5].wait_recv()
            self.cp[6].wait_recv()
            self.fwd(9, tuw, 128, "c")

        def finish(self):
            for i in (0, 7, 8, 9):
                self.cp[i].wait_recv()

    gh = Gather(hid_ref, hidf, SEM_GH)
    gc = Gather(cot_ref, cotf, SEM_GC)
    gh.start()

    lane = lax.broadcasted_iota(jnp.int32, (1, C), 1)
    for i in range(3):
        wcat[:, i * C:(i + 1) * C] = wqkv_ref[i]
        wcatT[i * C:(i + 1) * C, :] = wqkv_ref[i].T
    wdT[...] = wd_ref[...].T

    @pl.loop(0, 4)
    def _(i):
        r = pl.ds(pl.multiple_of(i * 128, 128), 128)
        wdnT[:, r] = wdn_ref[r, :].T
        wupT[r, :] = wup_ref[:, r].T

    freq = prm_ref[6:7, 0:C]
    sign = prm_ref[6:7, C:2 * C]

    @pl.loop(0, 8)
    def _(i):
        r = pl.ds(pl.multiple_of(i * 128, 128), 128)
        pcol = jnp.broadcast_to(pos_ref[0:1, r].astype(f32), (128, 128)).T
        phase = pcol * freq
        ct[r, :] = jnp.cos(phase)
        st[r, :] = jnp.sin(phase) * sign
        segc[r, :] = jnp.broadcast_to(seg_ref[0:1, r].astype(f32), (128, 128)).T

    gh.mid()
    gc.start()
    gh.d2d()
    gh.last()
    gh.finish()

    g1 = prm_ref[0:1, :]
    b1 = prm_ref[1:2, :]
    g2 = prm_ref[2:3, :]
    b2 = prm_ref[3:4, :]
    low8 = (lane % HD) < 8

    def partner(v):
        return jnp.where(low8, pltpu.roll(v, 120, 1), pltpu.roll(v, 8, 1))

    def norm_stats(xb):
        mu = jnp.mean(xb, axis=1, keepdims=True)
        xc = xb - mu
        rstd = lax.rsqrt(jnp.mean(xc * xc, axis=1, keepdims=True) + EPS)
        return xc * rstd, rstd

    def forward_rows(i):
        r = pl.ds(pl.multiple_of(i * 256, 256), 256)
        xhat, _ = norm_stats(hidf[r, :].astype(f32))
        xh[r, :] = xhat.astype(bf16)
        m1 = (xhat * g1 + b1).astype(bf16)
        m2 = (xhat * g2 + b2).astype(bf16)
        n1[r, :] = m1
        n2[r, :] = m2
        gate = dot(m2, wup_ref[...]) + prm_ref[5:6, 0:F]
        cdf = 0.5 * (1.0 + lax.erf(gate * 0.7071067811865476))
        act_s[r, :] = (gate * cdf).astype(bf16)
        gel[r, :] = cdf + gate * (jnp.exp(-0.5 * gate * gate) * 0.3989422804014327)
        pr = dot(m1, wcat[...]) + prm_ref[5:6, F:F + 3 * C]
        cb, sb = ct[r, :], st[r, :]
        qp, kp, vp = pr[:, 0:C], pr[:, C:2 * C], pr[:, 2 * C:]
        qs[r, :] = ((qp * cb + partner(qp) * sb) * 0.125).astype(bf16)
        kr = kp * cb + partner(kp) * sb
        ks[r, :] = kr.astype(bf16)
        vs[r, :] = vp.astype(bf16)
        kT[:, r] = kr.T.astype(bf16)
        vT[:, r] = vp.T.astype(bf16)

    pl.loop(0, 2)(forward_rows)
    gc.mid()
    pl.loop(2, 4)(forward_rows)
    gc.d2d()
    gc.last()
    gc.finish()

    smv[0] = jnp.zeros((8, D), f32)
    smv[0, 0:1, :] = jnp.sum(cot_ref[0].astype(f32), axis=0, keepdims=True)

    @pl.loop(0, 4)
    def _(i):
        r = pl.ds(pl.multiple_of(i * 256, 256), 256)
        cb = cotf[r, :]
        gb = (dot(cb, wdnT[...]) * gel[r, :]).astype(bf16)
        gg[r, :] = gb
        smv[0, 5:6, 0:F] += jnp.sum(gb.astype(f32), axis=0, keepdims=True)
        ga[r, :] = dot(cb, wdT[...]).astype(bf16)

    class AllReduce:
        def __init__(self, g, rr, o, base, n):
            self.g, self.r, self.o, self.b, self.n = g, rr, o, base, n
            self.off = {}
            self.cp = {}

        def rows(self, s):
            return self.n >> (s + 1)

        def start(self, s, qs_=range(4)):
            h = self.rows(s)
            for q in qs_:
                off = self.off[q, s] if s else 0
                b = bit[ORD[q][s]]
                self.off[q, s + 1] = pl.multiple_of(off + b * h, h)
                src = pl.multiple_of(off + (1 - b) * h, h)
                roff = self.n - 2 * h
                self.cp[q, s] = send(
                    self.b + q * 8 + s, self.g.at[q, pl.ds(src, h)], self.r.at[q, pl.ds(roff, h)], ORD[q][s]
                )

        def add(self, s, qs_=range(4)):
            h = self.rows(s)
            roff = self.n - 2 * h
            for q in qs_:
                self.cp[q, s].wait_recv()
                keep = pl.ds(self.off[q, s + 1], h)
                tot = self.g[q, keep, :].astype(f32) + self.r[q, pl.ds(roff, h), :].astype(f32)
                if s == 3:
                    self.o[q, keep, :] = tot.astype(bf16)
                else:
                    self.g[q, keep, :] = tot.astype(bf16)

        def step(self, s):
            self.add(s)
            if s < 3:
                self.start(s + 1)
            else:
                self.spread(3)

        def spread(self, s):
            h = self.rows(s)
            for q in range(4):
                ref = self.o.at[q, pl.ds(self.off[q, s + 1], h)]
                self.cp[q, 7 - s] = send(self.b + q * 8 + 7 - s, ref, ref, ORD[q][s])

        def back(self, s):
            for q in range(4):
                self.cp[q, 7 - s].wait_recv()
            if s > 0:
                self.spread(s - 1)

    arf = AllReduce(gf, rf, of_out, SEM_F, 256)
    arw = AllReduce(gw, rw, ow_out, SEM_W, 1024)

    for j in range(2):
        @pl.loop(0, 2)
        def _(i, j=j):
            cc = pl.ds(pl.multiple_of(i * 512, 512), 512)
            gf[j, :, cc] = dot_tn(act_s[:, j * 256:(j + 1) * 256], cotf[:, cc]).astype(bf16)

        arf.start(0, (j,))
    for j in range(2):
        @pl.loop(0, 2)
        def _(i, j=j):
            rr = pl.ds(pl.multiple_of(j * 512 + i * 256, 256), 256)
            cc = pl.ds(pl.multiple_of(i * 512, 512), 512)
            gf[2 + j, :, cc] = dot_tn(n2[:, rr], gg[...]).astype(bf16)

        arf.start(0, (2 + j,))

    @pl.loop(0, 4)
    def _(i):
        r = pl.ds(pl.multiple_of(i * 256, 256), 256)
        po[r, :] = dot(act_s[r, :], wdn_ref[...])
        g2c = dot(gg[r, :], wupT[...])
        smv[0, 3:4, :] += jnp.sum(g2c * xh[r, :].astype(f32), axis=0, keepdims=True)
        smv[0, 4:5, :] += jnp.sum(g2c, axis=0, keepdims=True)
        dxh[r, :] = g2c * g2

    arf.step(0)

    dk[...] = jnp.zeros_like(dk)
    dv[...] = jnp.zeros_like(dv)

    def attention_block(i):
        q0, L = i * 256, (i + 1) * 256
        qb, gb = qs[q0:L, :], ga[q0:L, :]
        zero = jnp.zeros((), bf16)
        kidx = lax.broadcasted_iota(jnp.int32, (L, 256), 0)
        qidx = lax.broadcasted_iota(jnp.int32, (L, 256), 1) + q0
        sc = segc[0:L, :]
        same = jnp.concatenate([sc, sc], axis=1) == seg_ref[0:1, q0:L].astype(f32)
        allowed = same & (kidx <= qidx)
        pbs, dss, qms, gms, outs, dqs = [], [], [], [], [], []
        for h in range(2):
            mine = (lane // HD) == h
            qm, gm = jnp.where(mine, qb, zero), jnp.where(mine, gb, zero)
            s = jnp.where(allowed, dot_nt(ks[0:L, :], qm), -1e30)
            e = jnp.exp(s - jnp.max(s, axis=0, keepdims=True))
            p = e / jnp.sum(e, axis=0, keepdims=True)
            pb = p.astype(bf16)
            dp_ = dot_nt(vs[0:L, :], gm)
            ds = (p * (dp_ - jnp.sum(p * dp_, axis=0, keepdims=True))).astype(bf16)
            outs.append(dot(vT[h * HD:(h + 1) * HD, 0:L], pb))
            dqs.append(dot(kT[h * HD:(h + 1) * HD, 0:L], ds))
            pbs.append(pb)
            dss.append(ds)
            qms.append(qm)
            gms.append(gm)
        dv[0:L, :] += dot(jnp.concatenate(pbs, axis=1), jnp.concatenate(gms, axis=0))
        dk[0:L, :] += dot(jnp.concatenate(dss, axis=1), jnp.concatenate(qms, axis=0))
        oT = jnp.concatenate(outs, axis=0)
        attT[:, q0:L] = oT.astype(bf16)
        att[q0:L, :] = oT.T.astype(bf16)
        dq = jnp.concatenate(dqs, axis=0).T
        dq = (dq * ct[q0:L, :] - partner(dq) * st[q0:L, :]) * 0.125
        gp[q0:L, 0:C] = dq.astype(bf16)

    attention_block(0)
    attention_block(1)
    arf.step(1)
    attention_block(2)
    arf.step(2)
    attention_block(3)
    arf.step(3)

    @pl.loop(0, 4)
    def _(i):
        r = pl.ds(pl.multiple_of(i * 256, 256), 256)
        dkb = dk[r, :]
        gp[r, C:2 * C] = (dkb * ct[r, :] - partner(dkb) * st[r, :]).astype(bf16)
        gp[r, 2 * C:] = dv[r, :].astype(bf16)
        smv[0, 5:6, F:F + 3 * C] += jnp.sum(gp[r, :].astype(f32), axis=0, keepdims=True)

    arf.back(3)

    @pl.loop(0, 4)
    def _(i):
        r = pl.ds(pl.multiple_of(i * 256, 256), 256)
        res = dot_tn(n1[:, r], gp[...]).astype(bf16)
        gw[0, r, :] = res[:, 0:C]
        gw[1, r, :] = res[:, C:2 * C]
        gw[2, r, :] = res[:, 2 * C:]
        dn = dot(attT[...], cotf[:, r]).astype(bf16)
        gw[3, pl.ds(pl.multiple_of(i * 256, 256), 128), :] = dn[:, 0:C]
        gw[3, pl.ds(pl.multiple_of(i * 256 + 128, 128), 128), :] = dn[:, C:]

    arw.start(0)
    arf.back(2)

    class Scatter:
        def __init__(self, full, s0, r0, ss, r1, r2, base):
            self.full, self.s0, self.r0, self.ss, self.r1, self.r2, self.b = full, s0, r0, ss, r1, r2, base
            self.cp = {}

        def give(self):
            for i in range(4):
                row = pl.multiple_of(i * 256 + (1 - c) * 128, 128)
                self.s0[i] = self.full[pl.ds(row, 128), :].astype(bf16)
                self.cp[i] = send(self.b + i, self.s0.at[i], self.r0.at[i], "c")

        def fold(self):
            for u in range(2):
                for w in range(2):
                    i = 2 * w + (u ^ w)
                    self.cp[i].wait_recv()
                    row = pl.multiple_of(i * 256 + c * 128, 128)
                    val = (self.full[pl.ds(row, 128), :] + self.r0[i].astype(f32)).astype(bf16)
                    self.ss[0, u, w] = val[0:64]
                    self.ss[1, w, u] = val[64:128]
            self.cp[4] = send(self.b + 4, self.ss.at[0, 1 - xu], self.r1.at[0], "xu")
            self.cp[5] = send(self.b + 5, self.ss.at[1, 1 - xw], self.r1.at[1], "xw")

        def second(self):
            self.cp[4].wait_recv()
            for w in range(2):
                self.r1[0, w] = (self.r1[0, w].astype(f32) + self.ss[0, xu, w].astype(f32)).astype(bf16)
            self.cp[6] = send(self.b + 6, self.r1.at[0, 1 - xw], self.r2.at[0], "xw")
            self.cp[5].wait_recv()
            for u in range(2):
                self.r1[1, u] = (self.r1[1, u].astype(f32) + self.ss[1, xw, u].astype(f32)).astype(bf16)
            self.cp[7] = send(self.b + 7, self.r1.at[1, 1 - xu], self.r2.at[1], "xu")

        def result(self, half):
            self.cp[6 + half].wait_recv()
            mine = self.r1[0, xw] if half == 0 else self.r1[1, xu]
            return mine.astype(f32) + self.r2[half].astype(f32)

    rsa = Scatter(po, sa, ra, ssa, r1a, r2a, SEM_RA)
    rsd = Scatter(dxh, sd, rd, ssd, r1d, r2d, SEM_RD)

    @pl.loop(0, 4)
    def _(i):
        r = pl.ds(pl.multiple_of(i * 256, 256), 256)
        g1c = dot(gp[r, :], wcatT[...])
        smv[0, 1:2, :] += jnp.sum(g1c * xh[r, :].astype(f32), axis=0, keepdims=True)
        smv[0, 2:3, :] += jnp.sum(g1c, axis=0, keepdims=True)
        dxh[r, :] += g1c * g1
        po[r, :] += dot(att[r, :], wd_ref[...])

    DIMS = YZ + ("xu", "xw", "c")
    smc = {}

    def small_start(k):
        smc[k] = send(SEM_S + k, smv.at[k], smr.at[k], DIMS[k])

    def small_step(k):
        smc[k].wait_recv()
        smv[k + 1] = smv[k] + smr[k]
        if k < 6:
            small_start(k + 1)

    small_start(0)
    rsa.give()
    rsd.give()
    arf.back(1)
    rsa.fold()
    rsd.fold()
    arw.step(0)
    small_step(0)
    rsa.second()
    arw.step(1)
    small_step(1)
    rsd.second()
    arw.step(2)
    small_step(2)

    for half in range(2):
        hr = pl.ds(half * 64, 64)
        act = hid_ref[0, hr, :].astype(f32) + rsa.result(half) + prm_ref[4:5, :]
        act_out[hr, :] = act.astype(bf16)
    arw.step(3)
    small_step(3)
    for half in range(2):
        hr = pl.ds(half * 64, 64)
        d = rsd.result(half)
        xhat, rstd = norm_stats(hid_ref[0, hr, :].astype(f32))
        back = (d - jnp.mean(d, axis=1, keepdims=True) - xhat * jnp.mean(d * xhat, axis=1, keepdims=True)) * rstd
        ing_out[hr, :] = cot_ref[0, hr, :].astype(f32) + back
    arw.back(3)
    small_step(4)
    arw.back(2)
    small_step(5)
    arw.back(1)
    small_step(6)
    arf.back(0)
    arw.back(0)
    sm_out[...] = smv[7]
    sm_out[5:6, :] = smv[4, 5:6, :]
    for cp in pending:
        cp.wait_send()


def layer(hid, cot, seg, pos, prm, wqkv, wd, wup, wdn):
    v = lambda s, d: pltpu.VMEM(s, d)
    big = (1024, 1024)
    scratch = [
        v(big, bf16), v(big, bf16), v(big, bf16), v(big, bf16), v(big, bf16),
        v((1024, F), bf16), v((1024, F), f32), v((1024, F), bf16),
        v((1024, C), bf16), v((1024, C), bf16), v((1024, C), bf16), v((1024, C), bf16),
        v((C, 1024), bf16), v((C, 1024), bf16), v((C, 1024), bf16), v((1024, C), bf16),
        v((1024, 3 * C), bf16),
        v((1024, C), f32), v((1024, C), f32),
        v((1024, 3 * C), bf16), v((3 * C, 1024), bf16), v((F, 1024), bf16), v((1024, F), bf16), v((1024, C), bf16),
        v((1024, C), f32), v((1024, C), f32), v((1024, C), f32),
        v(big, f32), v(big, f32),
        v((4, 256, 1024), bf16), v((4, 256, 1024), bf16), v((4, 1024, C), bf16), v((4, 1024, C), bf16),
    ]
    for _ in range(2):
        scratch += [
            v((4, 128, D), bf16), v((4, 128, D), bf16), v((2, 2, 2, 64, D), bf16), v((2, 2, 64, D), bf16),
            v((2, 64, D), bf16),
        ]
    scratch += [v((8, 8, D), f32), v((7, 8, D), f32)]
    scratch += [pltpu.SemaphoreType.DMA((NSEM,)), pltpu.SemaphoreType.DMA((NSEM,))]
    vm = pl.BlockSpec(memory_space=pltpu.VMEM)
    return pl.pallas_call(
        kernel_body,
        out_shape=[
            jax.ShapeDtypeStruct((128, D), bf16),
            jax.ShapeDtypeStruct((128, D), f32),
            jax.ShapeDtypeStruct((4, 256, 1024), bf16),
            jax.ShapeDtypeStruct((4, 1024, C), bf16),
            jax.ShapeDtypeStruct((8, D), f32),
        ],
        in_specs=[vm] * 9,
        out_specs=[vm] * 5,
        scratch_shapes=scratch,
        compiler_params=pltpu.CompilerParams(
            collective_id=0, has_side_effects=True, vmem_limit_bytes=63 * 1024 * 1024
        ),
    )(hid, cot, seg, pos, prm, wqkv, wd, wup, wdn)


def local(
    hidden_in, first_gain, first_shift, second_gain, second_shift, qkv_weight, qkv_bias, dense_weight,
    up_weight, up_bias, down_weight, out_bias, segments, positions, cotangent,
):
    freq = 10000.0 ** (-2.0 * jnp.arange(8, dtype=f32) / 16)
    zeros = jnp.zeros((48,), f32)
    head_freq = jnp.concatenate([freq, freq, zeros])
    head_sign = jnp.concatenate([-jnp.ones((8,), f32), jnp.ones((8,), f32), zeros])
    consts = jnp.concatenate([head_freq, head_freq, head_sign, head_sign, jnp.zeros((768,), f32)])
    biases = jnp.concatenate([up_bias, qkv_bias.reshape(3 * C), jnp.zeros((128,), bf16)]).astype(f32)
    rows = [first_gain, first_shift, second_gain, second_shift, out_bias]
    prm = jnp.stack([r.astype(f32) for r in rows] + [biases, consts, jnp.zeros((D,), f32)])
    act, ing, of, ow, sm = layer(
        hidden_in, cotangent, segments, positions, prm, qkv_weight, dense_weight, up_weight, down_weight
    )
    grad_down = of[0:2].reshape(F, D).astype(f32)
    grad_up = of[2:4].reshape(2, 256, 2, F).transpose(0, 2, 1, 3).reshape(D, F).astype(f32)
    grad_qkv = ow[0:3].astype(f32)
    grad_dense = ow[3].reshape(8, C, C).transpose(1, 0, 2).reshape(C, D).astype(f32)
    return (
        act[None], ing[None], grad_qkv, sm[5, F:F + 3 * C].reshape(3, C), grad_dense, grad_up, sm[5, 0:F],
        grad_down, sm[0], sm[1], sm[2], sm[3], sm[4],
    )


def solution(mesh):
    placed = (
        P("dp", "tensor", None), P(), P(), P(), P(), P(None, None, "tensor"), P(None, "tensor"),
        P("tensor", None), P(None, "tensor"), P("tensor"), P("tensor", None), P(), P("dp", None),
        P("dp", None), P("dp", "tensor", None),
    )
    return jax.shard_map(
        local,
        mesh=mesh,
        in_specs=placed,
        out_specs=(
            P("dp", "tensor", None), P("dp", "tensor", None), P(None, None, "tensor"), P(None, "tensor"),
            P("tensor", None), P(None, "tensor"), P("tensor"), P("tensor", None), P(), P(), P(), P(), P(),
        ),
        check_vma=False,
    )
```

time: 448 us -> 134 us (0.30)
  waiting for transfers between devices: 216 us -> 0 us
  Pallas kernels: 0 us -> 109 us
  blocking collectives: 108 us -> 0 us
  matrix products: 48.3 us -> 0 us
  other arithmetic: 24 us -> 9.01 us
  between operations: 14.7 us -> 0.71 us
  local copies, waits for them, and re-layouts: 27.6 us -> 14.6 us
  loops' own time: 6.69 us -> 0 us
    reduce_scatter x3 -> x0, waiting for transfers between devices: 112 us -> none  [the longest x1 39.3 us: local(): lax.psum_scatter(grad_norm_two.reshape(seq_count, SEQ, D), 'tensor', scat...]
    pallas_call x0 -> x1, Pallas kernels: none -> 109 us  [layer(): pl.pallas_call(kernel_body, out_shape=[jax.ShapeDtypeStruct((128, D), bf1...]
    psum x2 -> x0, blocking collectives: 108 us -> none  [the longest x1 65.7 us: local(): lax.psum((grad_gain_one, grad_shift_one, grad_gain_two, grad_shift_two, g...]
    psum x1 -> x0, waiting for transfers between devices: 66.1 us -> none  [local(): lax.psum((grad_qkv, grad_qkv_bias, grad_dense, grad_up, grad_up_bias, gra...]
    dot_general x25 -> x0, matrix products: 45.6 us -> none  [the longest x1 7.26 us: local(): jnp.dot(flat_two, up_weight, preferred_element_type=jnp.float32)]
    all_gather x3 -> x0, waiting for transfers between devices: 36.7 us -> none  [the longest x1 24.7 us: local(): lax.all_gather(low_one, 'tensor', axis=1, tiled=True)]
    unnamed x88 -> x9, local copies, waits for them, and re-layouts: 16.1 us -> 2.19 us
    reduce_sum x8 -> x0, other arithmetic: 10.2 us -> none  [the longest x2 3.3 us: layer_norm(): return centered * lax.rsqrt(spread + norm_epsilon) * norm_gain + norm_shift]
  transfers between devices with their start and end apart: 7 -> 0, of which waited for: 6 -> 0; matrix products, arithmetic and copies ran while one was open for 13% -> 0% of each run, Pallas kernels for 0% -> 0%
where the time goes in v1:
time: 134 us; the launch traced here: 133 us
  Pallas kernels  109 us (81%)
  local copies, waits for them, and re-layouts  14.6 us (11%)
  other arithmetic  9.01 us (7%)
    pallas_call x1, Pallas kernels, layer(): pl.pallas_call(kernel_body, out_shape=[jax.ShapeDtypeStruct((128, D), bf1...  109 us
    convert_element_type x2, local copies, waits for them, and re-layouts, local(): of[2:4].reshape(2, 256, 2, F).transpose(0, 2, 1, 3).reshape(D, F)  6.09 us
    another operation x5, other arithmetic, local(): jnp.stack([r.astype(f32) for r in rows] + [biases, consts, jnp.zeros((D,)...  3.42 us

profile of v1, /device:TPU:0, one launch (start us, length us, event | category | flops | bytes accessed | tf_op | source)
XLA Modules:
  0.0 133.2 jit_solution(7839609767607122474)
XLA Ops:
  0.7 0.7 concatenate.19
  1.4 0.7 copy.34
  2.1 0.8 concatenate.22
  2.9 0.7 stack.49
  3.6 0.7 stack.50
  4.3 0.7 stack.51
  4.9 0.7 stack.52
  5.6 0.7 stack.53
  6.3 0.7 stack.48.prm_ref
  7.0 108.9 %shard_map.246 = (bf16[128,1024]{1,0:T(8,128)(2,1)}, f32[128,1024]{1,0:T(8,128)}, bf16[4,256,1024]{2,1,0:T(8,128)(2,1)}, bf16[4,1024,128]{2,1,0:T(8,128)(2,1)}, f32[8,1024]{1,0:T(8,128)}) custom-call(bf16[1,128,1024]{2,1,0:T(8,128)(2,1)} %hid_ref.1, bf16[1,128,1024]{2,1,0:T(8,128)(2,1)} %cot_ref.1, s32[1,1024]{1,0:T(1,128)} %seg_ref.1, s32[1,1024]{1,0:T(1,128)} %pos_ref.1, ...), custom_call_target="tpu_custom_call" | custom-call | tf_op jit(solution)/shard_map/pallas_call | solution.py:509
  115.9 1.6 %fusion.2 = (f32[1,1024]{1,0:T(1,128)}, f32[1,1024]{1,0:T(1,128)}, f32[1,1024]{1,0:T(1,128)}, f32[1,1024]{1,0:T(1,128)}, f32[1,1024]{1,0:T(1,128)}) fusion(f32[8,1024]{1,0:T(8,128)} %get-tuple-element.21), kind=kLoop, calls=%fused_computation.11 | loop fusion | bytes 40960 | tf_op jit(solution)/shard_map/slice | solution.py:548
  117.4 1.3 slice.37
  118.7 1.3 slice_reduce_fusion
  120.0 1.9 %fusion.1 = (bf16[2,256,1024]{2,1,0:T(8,128)(2,1)S(1)}, f32[2,256,1024]{2,1,0:T(8,128)S(1)}) fusion(bf16[4,256,1024]{2,1,0:T(8,128)(2,1)} %get-tuple-element.22), kind=kLoop, calls=%fused_computation.10 | loop fusion | flops 524288 | bytes 5242880 | tf_op jit(solution)/shard_map/slice | solution.py:542
  121.9 2.8 %reshape.87 = f32[2,256,2,512]{3,2,1,0:T(2,128)} reshape(f32[2,256,1024]{2,1,0:T(8,128)S(1)} %get-tuple-element.24) | data formatting | bytes 4194304 | tf_op jit(solution)/shard_map/convert_element_type | solution.py:543
  124.7 3.3 %copy.29 = f32[2,2,256,512]{3,2,1,0:T(8,128)} copy(f32[2,2,256,512]{3,1,2,0:T(2,128)} %bitcast.33) | data formatting | bytes 4194304 | tf_op jit(solution)/shard_map/convert_element_type | solution.py:543
  128.0 0.0 copy-start
  128.0 1.6 %bitcast_convert_fusion = f32[512,1024]{1,0:T(8,128)} fusion(bf16[2,256,1024]{2,1,0:T(8,128)(2,1)S(1)} %get-tuple-element.23), kind=kLoop, calls=%fused_computation | loop fusion | flops 524288 | bytes 3145728 | tf_op jit(solution)/shard_map/convert_element_type | solution.py:542
  129.6 0.0 copy-start.2
  129.6 0.0 copy-done
  129.6 0.0 copy-start.1
  129.6 1.2 slice_convert_fusion.1
  130.9 0.8 copy_bitcast_fusion
  131.7 0.0 copy-done.2
  131.7 0.7 copy.37
  132.4 0.0 copy-done.1
  132.4 0.8 copy.38
  (8 shorter events, 0.1 us)
Async XLA Ops:
  128.0 1.6 %copy-start = (bf16[4,1024,128]{2,1,0:T(8,128)(2,1)S(1)}, bf16[4,1024,128]{2,1,0:T(8,128)(2,1)}, u32[]{:S(2)}) copy-start(bf16[4,1024,128]{2,1,0:T(8,128)(2,1)} %get-tuple-element.20) | copy-start | bytes 3145732
  129.6 2.1 %copy-start.2 = (bf16[128,1024]{1,0:T(8,128)(2,1)S(1)}, bf16[128,1024]{1,0:T(8,128)(2,1)}, u32[]{:S(2)}) copy-start(bf16[128,1024]{1,0:T(8,128)(2,1)} %get-tuple-element.18) | copy-start | bytes 786436
  129.6 2.8 %copy-start.1 = (f32[128,1024]{1,0:T(8,128)S(1)}, f32[128,1024]{1,0:T(8,128)}, u32[]{:S(2)}) copy-start(f32[128,1024]{1,0:T(8,128)} %get-tuple-element.19) | copy-start | bytes 1572868

commit v2 on v1

v2 whole, which is shorter than its diff:
```python
import jax
import jax.numpy as jnp
from jax import lax
from jax.experimental import pallas as pl
from jax.experimental.pallas import tpu as pltpu
from jax.sharding import PartitionSpec as P

D = 1024
HD = 64
SEQ = 1024
F = 512
C = 128
EPS = 1e-05
f32 = jnp.float32
bf16 = jnp.bfloat16
NSEM = 176

YZ = ("yu", "yw", "zu", "zw")
ORD = tuple(tuple(YZ[(q + s) % 4] for s in range(4)) for q in range(4))


def dot(a, b):
    return lax.dot_general(a, b, (((1,), (0,)), ((), ())), preferred_element_type=f32)


def dot_nt(a, b):
    return lax.dot_general(a, b, (((1,), (1,)), ((), ())), preferred_element_type=f32)


def dot_tn(a, b):
    return lax.dot_general(a, b, (((0,), (0,)), ((), ())), preferred_element_type=f32)


def column(row, n):
    return jnp.broadcast_to(row.astype(f32), (n, row.shape[1])).T


def kernel_body(
    hid_ref, cot_ref, seg_ref, pos_ref, g1_ref, b1_ref, g2_ref, b2_ref, ob_ref, ub_ref, qb_ref,
    wqkv_ref, wd_ref, wup_ref, wdn_ref,
    act_out, ing_out, od_out, ou_out, ow_out, sm_out,
    hidf, cotf, xh, n1, n2, act_s, gel, gg, qs, ks, vs, ga, vT, kT, attT, att, gp,
    dk, dv, wqkv, wd, wup, wdn, wcat, wcatT, wupT, wdnT, wdT, ct, st, segc, po, dxh,
    gd, rd_, od, gu, ru_, ou, gw, rw1, pw, rw2, ow,
    sa, ra, ssa, r1a, r2a, sd, rd, ssd, r1d, r2d, sm, smy, smz, smt,
    ssem, rsem, lsem,
):
    dp = lax.axis_index("dp")
    tn = lax.axis_index("tensor")
    c = tn % 2
    x = tn // 2
    y = dp % 4
    z = dp // 4

    def flip(v):
        return v + 1 - 2 * (v % 2)

    def ub(v):
        return (v + v // 2) % 2

    def wb(v):
        return v // 2

    peer = {
        "c": (dp, x * 2 + 1 - c),
        "xu": (dp, flip(x) * 2 + c),
        "xw": (dp, (3 - x) * 2 + c),
        "yu": (z * 4 + flip(y), tn),
        "yw": (z * 4 + 3 - y, tn),
        "zu": (flip(z) * 4 + y, tn),
        "zw": ((3 - z) * 4 + y, tn),
    }
    ring = []
    for k in range(1, 4):
        peer["y", k] = (z * 4 + (y + k) % 4, tn)
        peer["z", k] = (((z + k) % 4) * 4 + y, tn)
        ring += [("y", k), ("z", k)]
    for k in range(1, 8):
        peer["t", k] = (dp, (tn + k) % 8)
        ring.append(("t", k))
    bit = {"yu": ub(y), "yw": wb(y), "zu": ub(z), "zw": wb(z)}
    xu, xw = ub(x), wb(x)

    pending = []
    count = [0]

    def send(src, dst, who):
        i = count[0]
        count[0] += 1
        cp = pltpu.make_async_remote_copy(
            src_ref=src, dst_ref=dst, send_sem=ssem.at[i], recv_sem=rsem.at[i],
            device_id=peer[who], device_id_type=pl.DeviceIdType.MESH,
        )
        cp.start()
        pending.append(cp)
        return cp

    own = pl.multiple_of(tn * 128, 128)
    own_rows = pl.ds(own, 128)
    moves = []

    def move(src, dst):
        cp = pltpu.make_async_copy(src, dst, lsem.at[len(moves)])
        cp.start()
        moves.append(cp)
        return cp

    m_hid = move(hid_ref.at[0], hidf.at[own_rows])
    m_cot = move(cot_ref.at[0], cotf.at[own_rows])
    m_w = [move(wqkv_ref, wqkv), move(wd_ref, wd), move(wup_ref, wup), move(wdn_ref, wdn)]

    barrier = pltpu.get_barrier_semaphore()
    for who in ring:
        pl.semaphore_signal(barrier, inc=1, device_id=peer[who], device_id_type=pl.DeviceIdType.MESH)
    pl.semaphore_wait(barrier, len(ring))

    x2 = flip(3 - x)
    tu = pl.multiple_of((flip(x) * 2 + c) * 128, 128)
    tw = pl.multiple_of(((3 - x) * 2 + c) * 128, 128)
    tuw = pl.multiple_of((x2 * 2 + c) * 128, 128)
    row_own = pl.multiple_of(x * 256, 256)
    row_u = pl.multiple_of(flip(x) * 256, 256)
    row_w = pl.multiple_of((3 - x) * 256, 256)
    row_uw = pl.multiple_of(x2 * 256, 256)

    class Gather:
        def __init__(self, src, full):
            self.src, self.full, self.cp = src, full, {}

        def fwd(self, i, row, n, who):
            ref = self.full.at[pl.ds(row, n)]
            self.cp[i] = send(ref, ref, who)

        def start_core(self):
            self.cp[0] = send(self.src.at[0], self.full.at[own_rows], "c")

        def start(self):
            lo, hi = self.src.at[0, pl.ds(0, 64)], self.src.at[0, pl.ds(64, 64)]
            dlo, dhi = self.full.at[pl.ds(own, 64)], self.full.at[pl.ds(own + 64, 64)]
            self.cp[1] = send(lo, dlo, "xu")
            self.cp[2] = send(hi, dhi, "xw")
            self.cp[3] = send(hi, dhi, "xu")
            self.cp[4] = send(lo, dlo, "xw")

        def mid(self):
            self.cp[1].wait_recv()
            self.fwd(5, tu, 64, "xw")
            self.cp[2].wait_recv()
            self.fwd(6, tw + 64, 64, "xu")

        def d2d(self):
            self.cp[3].wait_recv()
            self.fwd(7, tu, 128, "c")
            self.cp[4].wait_recv()
            self.fwd(8, tw, 128, "c")

        def last(self):
            self.cp[5].wait_recv()
            self.cp[6].wait_recv()
            self.fwd(9, tuw, 128, "c")

        def ready(self, i):
            self.cp[i].wait_recv()

    gh = Gather(hid_ref, hidf)
    gc = Gather(cot_ref, cotf)
    gh.start()
    gh.start_core()

    lane = lax.broadcasted_iota(jnp.int32, (1, C), 1)
    turn = lane % 8
    freq = jnp.zeros((1, C), f32)
    for j in range(8):
        freq = jnp.where(turn == j, 10000.0 ** (-2.0 * j / 16), freq)
    place = lane % HD
    freq = jnp.where(place < 16, freq, 0.0)
    sign = jnp.where(place < 8, -1.0, 1.0)
    low8 = place < 8

    @pl.loop(0, 8)
    def _(i):
        r = pl.ds(pl.multiple_of(i * 128, 128), 128)
        phase = column(pos_ref[0:1, r], 128) * freq
        ct[r, :] = jnp.cos(phase)
        st[r, :] = jnp.sin(phase) * sign
        segc[r, :] = column(seg_ref[0:1, r], 128)

    for cp in m_w:
        cp.wait()
    m_hid.wait()
    m_cot.wait()
    for i in range(3):
        wcat[:, i * C:(i + 1) * C] = wqkv[i]
        wcatT[i * C:(i + 1) * C, :] = wqkv[i].T

    gh.mid()
    gc.start()
    gc.start_core()

    wdT[...] = wd[...].T

    @pl.loop(0, 4)
    def _(i):
        r = pl.ds(pl.multiple_of(i * 128, 128), 128)
        wdnT[:, r] = wdn[r, :].T
        wupT[r, :] = wup[:, r].T

    def row_of(ref):
        return ref[...].astype(f32).reshape(1, -1)

    g1, b1, g2, b2 = row_of(g1_ref), row_of(b1_ref), row_of(g2_ref), row_of(b2_ref)
    up_b = row_of(ub_ref)
    qb_all = qb_ref[...].astype(f32)
    qkv_b = jnp.concatenate([qb_all[i:i + 1] for i in range(3)], axis=1)

    def partner(v):
        return jnp.where(low8, pltpu.roll(v, 120, 1), pltpu.roll(v, 8, 1))

    def norm_stats(xb):
        mu = jnp.mean(xb, axis=1, keepdims=True)
        xc = xb - mu
        rstd = lax.rsqrt(jnp.mean(xc * xc, axis=1, keepdims=True) + EPS)
        return xc * rstd, rstd

    def forward_rows(base):
        r = pl.ds(base, 256)
        xhat, _ = norm_stats(hidf[r, :].astype(f32))
        xh[r, :] = xhat.astype(bf16)
        m1 = (xhat * g1 + b1).astype(bf16)
        m2 = (xhat * g2 + b2).astype(bf16)
        n1[r, :] = m1
        n2[r, :] = m2
        gate = dot(m2, wup[...]) + up_b
        cdf = 0.5 * (1.0 + lax.erf(gate * 0.7071067811865476))
        act_s[r, :] = (gate * cdf).astype(bf16)
        gel[r, :] = cdf + gate * (jnp.exp(-0.5 * gate * gate) * 0.3989422804014327)
        pr = dot(m1, wcat[...]) + qkv_b
        cb, sb = ct[r, :], st[r, :]
        qp, kp, vp = pr[:, 0:C], pr[:, C:2 * C], pr[:, 2 * C:]
        qs[r, :] = ((qp * cb + partner(qp) * sb) * 0.125).astype(bf16)
        kr = kp * cb + partner(kp) * sb
        ks[r, :] = kr.astype(bf16)
        vs[r, :] = vp.astype(bf16)
        kT[:, r] = kr.T.astype(bf16)
        vT[:, r] = vp.T.astype(bf16)

    def backward_rows(base):
        r = pl.ds(base, 256)
        cb = cotf[r, :]
        gb = (dot(cb, wdnT[...]) * gel[r, :]).astype(bf16)
        gg[r, :] = gb
        sm[5:6, 0:F] += jnp.sum(gb.astype(f32), axis=0, keepdims=True)
        ga[r, :] = dot(cb, wdT[...]).astype(bf16)

    sm[...] = jnp.zeros((8, D), f32)
    sm[0:1, :] = jnp.sum(cotf[own_rows, :].astype(f32), axis=0, keepdims=True)

    gh.ready(0)
    forward_rows(row_own)
    gh.d2d()
    gh.ready(7)
    forward_rows(row_u)
    gh.last()
    gh.ready(8)
    forward_rows(row_w)
    gc.mid()
    gh.ready(9)
    forward_rows(row_uw)
    gc.d2d()
    gc.ready(0)
    backward_rows(row_own)
    gc.last()
    gc.ready(7)
    backward_rows(row_u)
    gc.ready(8)
    backward_rows(row_w)
    gc.ready(9)

    class AllReduce:
        def __init__(self, g, rr, o, n):
            self.g, self.r, self.o, self.n = g, rr, o, n
            self.off = {}
            self.cp = {}

        def rows(self, s):
            return self.n >> (s + 1)

        def start(self, s, qs_=range(4)):
            h = self.rows(s)
            for q in qs_:
                off = self.off[q, s] if s else 0
                b = bit[ORD[q][s]]
                self.off[q, s + 1] = pl.multiple_of(off + b * h, h)
                src = pl.multiple_of(off + (1 - b) * h, h)
                roff = self.n - 2 * h
                self.cp[q, s] = send(self.g.at[q, pl.ds(src, h)], self.r.at[q, pl.ds(roff, h)], ORD[q][s])

        def step(self, s):
            h = self.rows(s)
            roff = self.n - 2 * h
            for q in range(4):
                self.cp[q, s].wait_recv()
                keep = pl.ds(self.off[q, s + 1], h)
                tot = (self.g[q, keep, :].astype(f32) + self.r[q, pl.ds(roff, h), :].astype(f32)).astype(bf16)
                if s == 3:
                    self.o[q, keep, :] = tot
                    self.spread(3, (q,))
                else:
                    self.g[q, keep, :] = tot
                    self.start(s + 1, (q,))

        def spread(self, s, qs_=range(4)):
            h = self.rows(s)
            for q in qs_:
                ref = self.o.at[q, pl.ds(self.off[q, s + 1], h)]
                self.cp[q, 7 - s] = send(ref, ref, ORD[q][s])

        def back(self, s):
            for q in range(4):
                self.cp[q, 7 - s].wait_recv()
                if s > 0:
                    self.spread(s - 1, (q,))

    ard = AllReduce(gd, rd_, od, 256)
    aru = AllReduce(gu, ru_, ou, 256)

    for q in range(4):
        f0, d0 = 256 * (q // 2), 512 * (q % 2)
        gd[q] = dot_tn(act_s[:, f0:f0 + 256], cotf[:, d0:d0 + 512]).astype(bf16)
        ard.start(0, (q,))
    backward_rows(row_uw)
    for q in range(4):
        gu[q] = dot_tn(n2[:, 256 * q:256 * (q + 1)], gg[...]).astype(bf16)
        aru.start(0, (q,))

    dk[...] = jnp.zeros_like(dk)
    dv[...] = jnp.zeros_like(dv)

    def attention_block(i):
        q0, L = i * 256, (i + 1) * 256
        qb, gb = qs[q0:L, :], ga[q0:L, :]
        zero = jnp.zeros((), bf16)
        kidx = lax.broadcasted_iota(jnp.int32, (L, 256), 0)
        qidx = lax.broadcasted_iota(jnp.int32, (L, 256), 1) + q0
        sc = segc[0:L, :]
        same = jnp.concatenate([sc, sc], axis=1) == seg_ref[0:1, q0:L].astype(f32)
        allowed = same & (kidx <= qidx)
        pbs, dss, qms, gms, outs, dqs = [], [], [], [], [], []
        for h in range(2):
            mine = (lane // HD) == h
            qm, gm = jnp.where(mine, qb, zero), jnp.where(mine, gb, zero)
            s = jnp.where(allowed, dot_nt(ks[0:L, :], qm), -1e30)
            e = jnp.exp(s - jnp.max(s, axis=0, keepdims=True))
            p = e * (1.0 / jnp.sum(e, axis=0, keepdims=True))
            pb = p.astype(bf16)
            dp_ = dot_nt(vs[0:L, :], gm)
            ds = (p * (dp_ - jnp.sum(p * dp_, axis=0, keepdims=True))).astype(bf16)
            outs.append(dot(vT[h * HD:(h + 1) * HD, 0:L], pb))
            dqs.append(dot(kT[h * HD:(h + 1) * HD, 0:L], ds))
            pbs.append(pb)
            dss.append(ds)
            qms.append(qm)
            gms.append(gm)
        dv[0:L, :] += dot(jnp.concatenate(pbs, axis=1), jnp.concatenate(gms, axis=0))
        dk[0:L, :] += dot(jnp.concatenate(dss, axis=1), jnp.concatenate(qms, axis=0))
        oT = jnp.concatenate(outs, axis=0)
        attT[:, q0:L] = oT.astype(bf16)
        att[q0:L, :] = oT.T.astype(bf16)
        cb, sb = ct[q0:L, :], st[q0:L, :]
        dq = jnp.concatenate(dqs, axis=0).T
        gp[q0:L, 0:C] = ((dq * cb - partner(dq) * sb) * 0.125).astype(bf16)
        dkb = dk[q0:L, :]
        gp[q0:L, C:2 * C] = (dkb * cb - partner(dkb) * sb).astype(bf16)
        gp[q0:L, 2 * C:] = dv[q0:L, :].astype(bf16)
        sm[5:6, F:F + 3 * C] += jnp.sum(gp[q0:L, :].astype(f32), axis=0, keepdims=True)

    attention_block(3)
    ard.step(0)
    aru.step(0)
    attention_block(2)
    ard.step(1)
    aru.step(1)
    attention_block(1)
    ard.step(2)
    aru.step(2)
    attention_block(0)

    class RingReduce:
        def __init__(self):
            self.ax = (("y", y, "z", z), ("z", z, "y", y))
            self.cp = {}

        def start(self, a):
            ax, me, _, _ = self.ax[a]
            for k in (2, 1, 3):
                to = pl.multiple_of((me + k) % 4 * 256, 256)
                self.cp[a, 0, k] = send(gw.at[pl.ds(2 * a, 2), pl.ds(to, 256)], rw1.at[a, k - 1], (ax, k))

        def step1(self, a):
            _, me, ax, other = self.ax[a]
            for k in (1, 3, 2):
                self.cp[a, 0, k].wait_recv()
            tot = gw[pl.ds(2 * a, 2), pl.ds(pl.multiple_of(me * 256, 256), 256), :].astype(f32)
            for k in range(3):
                tot = tot + rw1[a, k].astype(f32)
            pw[a] = tot.astype(bf16)
            for k in (2, 1, 3):
                to = pl.multiple_of((other + k) % 4 * 64, 64)
                self.cp[a, 1, k] = send(pw.at[a, :, pl.ds(to, 64)], rw2.at[a, k - 1], (ax, k))

        def step2(self, a):
            _, me, ax, other = self.ax[a]
            for k in (1, 3, 2):
                self.cp[a, 1, k].wait_recv()
            tot = pw[a, :, pl.ds(pl.multiple_of(other * 64, 64), 64), :].astype(f32)
            for k in range(3):
                tot = tot + rw2[a, k].astype(f32)
            mine = pl.ds(pl.multiple_of(me * 256 + other * 64, 64), 64)
            ow[pl.ds(2 * a, 2), mine, :] = tot.astype(bf16)
            ref = ow.at[pl.ds(2 * a, 2), mine]
            for k in (2, 1, 3):
                self.cp[a, 2, k] = send(ref, ref, (ax, k))

        def step3(self, a):
            ax, me, _, _ = self.ax[a]
            for k in (1, 3, 2):
                self.cp[a, 2, k].wait_recv()
            ref = ow.at[pl.ds(2 * a, 2), pl.ds(pl.multiple_of(me * 256, 256), 256)]
            for k in (2, 1, 3):
                self.cp[a, 3, k] = send(ref, ref, (ax, k))

        def finish(self, a):
            for k in (1, 3, 2):
                self.cp[a, 3, k].wait_recv()

    arw = RingReduce()

    @pl.loop(0, 4)
    def _(i):
        r = pl.ds(pl.multiple_of(i * 256, 256), 256)
        res = dot_tn(n1[:, r], gp[...]).astype(bf16)
        gw[0, r, :] = res[:, 0:C]
        gw[1, r, :] = res[:, C:2 * C]
        gw[2, r, :] = res[:, 2 * C:]
        dn = dot(attT[...], cotf[:, r]).astype(bf16)
        gw[3, pl.ds(pl.multiple_of(i * 256, 256), 128), :] = dn[:, 0:C]
        gw[3, pl.ds(pl.multiple_of(i * 256 + 128, 128), 128), :] = dn[:, C:]

    arw.start(0)
    arw.start(1)
    ard.step(3)
    aru.step(3)

    class Scatter:
        def __init__(self, full, s0, r0, ss, r1, r2):
            self.full, self.s0, self.r0, self.ss, self.r1, self.r2 = full, s0, r0, ss, r1, r2
            self.cp = {}

        def give(self, i):
            row = pl.multiple_of(i * 256 + (1 - c) * 128, 128)
            self.s0[i] = self.full[pl.ds(row, 128), :].astype(bf16)
            self.cp[i] = send(self.s0.at[i], self.r0.at[i], "c")

        def fold(self):
            for u in range(2):
                for w in range(2):
                    i = 2 * w + (u ^ w)
                    self.cp[i].wait_recv()
                    row = pl.multiple_of(i * 256 + c * 128, 128)
                    val = (self.full[pl.ds(row, 128), :] + self.r0[i].astype(f32)).astype(bf16)
                    self.ss[0, u, w] = val[0:64]
                    self.ss[1, w, u] = val[64:128]
            self.cp[4] = send(self.ss.at[0, 1 - xu], self.r1.at[0], "xu")
            self.cp[5] = send(self.ss.at[1, 1 - xw], self.r1.at[1], "xw")

        def second(self):
            self.cp[4].wait_recv()
            for w in range(2):
                self.r1[0, w] = (self.r1[0, w].astype(f32) + self.ss[0, xu, w].astype(f32)).astype(bf16)
            self.cp[6] = send(self.r1.at[0, 1 - xw], self.r2.at[0], "xw")
            self.cp[5].wait_recv()
            for u in range(2):
                self.r1[1, u] = (self.r1[1, u].astype(f32) + self.ss[1, xw, u].astype(f32)).astype(bf16)
            self.cp[7] = send(self.r1.at[1, 1 - xu], self.r2.at[1], "xu")

        def result(self, half):
            self.cp[6 + half].wait_recv()
            mine = self.r1[0, xw] if half == 0 else self.r1[1, xu]
            return mine.astype(f32) + self.r2[half].astype(f32)

    rsa = Scatter(po, sa, ra, ssa, r1a, r2a)
    rsd = Scatter(dxh, sd, rd, ssd, r1d, r2d)

    for i in range(4):
        r = pl.ds(i * 256, 256)
        po[r, :] = dot(act_s[r, :], wdn[...]) + dot(att[r, :], wd[...])
        rsa.give(i)
    ard.back(3)
    aru.back(3)
    for i in range(4):
        r = pl.ds(i * 256, 256)
        xhb = xh[r, :].astype(f32)
        g1c = dot(gp[r, :], wcatT[...])
        sm[1:2, :] += jnp.sum(g1c * xhb, axis=0, keepdims=True)
        sm[2:3, :] += jnp.sum(g1c, axis=0, keepdims=True)
        dxh[r, :] = g1c * g1
        g2c = dot(gg[r, :], wupT[...])
        sm[3:4, :] += jnp.sum(g2c * xhb, axis=0, keepdims=True)
        sm[4:5, :] += jnp.sum(g2c, axis=0, keepdims=True)
        dxh[r, :] += g2c * g2
        rsd.give(i)
        if i == 1:
            ard.back(2)
            aru.back(2)

    small = {}

    def small_send(ax, n, src, buf, slot):
        buf[slot] = src
        for k in range(1, n):
            small[ax, k] = send(buf.at[slot], buf.at[slot], (ax, k))

    def small_sum(ax, n, buf):
        for k in range(1, n):
            small[ax, k].wait_recv()
        tot = buf[0]
        for k in range(1, n):
            tot = tot + buf[k]
        return tot

    small_send("y", 4, sm[...], smy, y)
    arw.step1(0)
    arw.step1(1)
    rsa.fold()
    ard.back(1)
    aru.back(1)
    arw.step2(0)
    arw.step2(1)
    rsd.fold()
    small_send("z", 4, small_sum("y", 4, smy), smz, z)
    arw.step3(0)
    arw.step3(1)
    rsa.second()
    rsd.second()
    tot_dp = small_sum("z", 4, smz)
    sm_out[5:6, :] = tot_dp[5:6]
    small_send("t", 8, tot_dp, smt, tn)
    ard.back(0)
    move(od, od_out)
    aru.back(0)
    move(ou, ou_out)

    out_b = row_of(ob_ref)
    for half in range(2):
        hr = pl.ds(half * 64, 64)
        hb = hidf[pl.ds(pl.multiple_of(own + half * 64, 64), 64), :].astype(f32)
        act_out[hr, :] = (hb + rsa.result(half) + out_b).astype(bf16)
    for half in range(2):
        hr = pl.ds(half * 64, 64)
        fr = pl.ds(pl.multiple_of(own + half * 64, 64), 64)
        d = rsd.result(half)
        xhat, rstd = norm_stats(hidf[fr, :].astype(f32))
        back = (d - jnp.mean(d, axis=1, keepdims=True) - xhat * jnp.mean(d * xhat, axis=1, keepdims=True)) * rstd
        ing_out[hr, :] = cotf[fr, :].astype(f32) + back
    sm_out[0:5, :] = small_sum("t", 8, smt)[0:5]
    sm_out[6:8, :] = jnp.zeros((2, D), f32)
    arw.finish(0)
    arw.finish(1)
    move(ow, ow_out)
    for cp in pending:
        cp.wait_send()
    for cp in moves[-3:]:
        cp.wait()


def layer(*args):
    v = lambda s, d: pltpu.VMEM(s, d)
    big = (1024, 1024)
    scratch = [
        v(big, bf16), v(big, bf16), v(big, bf16), v(big, bf16), v(big, bf16),
        v((1024, F), bf16), v((1024, F), f32), v((1024, F), bf16),
        v((1024, C), bf16), v((1024, C), bf16), v((1024, C), bf16), v((1024, C), bf16),
        v((C, 1024), bf16), v((C, 1024), bf16), v((C, 1024), bf16), v((1024, C), bf16),
        v((1024, 3 * C), bf16),
        v((1024, C), f32), v((1024, C), f32),
        v((3, 1024, C), bf16), v((C, D), bf16), v((D, F), bf16), v((F, D), bf16),
        v((1024, 3 * C), bf16), v((3 * C, 1024), bf16), v((F, 1024), bf16), v((1024, F), bf16), v((1024, C), bf16),
        v((1024, C), f32), v((1024, C), f32), v((1024, C), f32),
        v(big, f32), v(big, f32),
    ]
    for _ in range(2):
        scratch += [v((4, 256, F), bf16), v((4, 256, F), bf16), v((4, 256, F), bf16)]
    scratch += [
        v((4, 1024, C), bf16), v((2, 3, 2, 256, C), bf16), v((2, 2, 256, C), bf16), v((2, 3, 2, 64, C), bf16),
        v((4, 1024, C), bf16),
    ]
    for _ in range(2):
        scratch += [
            v((4, 128, D), bf16), v((4, 128, D), bf16), v((2, 2, 2, 64, D), bf16), v((2, 2, 64, D), bf16),
            v((2, 64, D), bf16),
        ]
    scratch += [v((8, D), f32), v((4, 8, D), f32), v((4, 8, D), f32), v((8, 8, D), f32)]
    scratch += [pltpu.SemaphoreType.DMA((NSEM,)), pltpu.SemaphoreType.DMA((NSEM,)), pltpu.SemaphoreType.DMA((12,))]
    vm = pl.BlockSpec(memory_space=pltpu.VMEM)
    hbm = pl.BlockSpec(memory_space=pl.ANY)
    return pl.pallas_call(
        kernel_body,
        out_shape=[
            jax.ShapeDtypeStruct((128, D), bf16),
            jax.ShapeDtypeStruct((128, D), f32),
            jax.ShapeDtypeStruct((4, 256, F), bf16),
            jax.ShapeDtypeStruct((4, 256, F), bf16),
            jax.ShapeDtypeStruct((4, 1024, C), bf16),
            jax.ShapeDtypeStruct((8, D), f32),
        ],
        in_specs=[hbm, hbm] + [vm] * 9 + [hbm] * 4,
        out_specs=[vm, vm, hbm, hbm, hbm, vm],
        scratch_shapes=scratch,
        compiler_params=pltpu.CompilerParams(
            collective_id=0, has_side_effects=True, vmem_limit_bytes=63 * 1024 * 1024
        ),
    )(*args)


def widen_body(
    act_ref, ing_ref, od_ref, ou_ref, ow_ref, sm_ref,
    act_out, ing_out, gq_out, gqb_out, gdn_out, gup_out, gub_out, gdown_out, ob_out, g1_out, b1_out, g2_out, b2_out,
    dbuf, ubuf, qbuf, nbuf, sem,
):
    copies = []

    def put(src, dst):
        cp = pltpu.make_async_copy(src, dst, sem.at[len(copies)])
        cp.start()
        copies.append(cp)

    put(act_ref, act_out.at[0])
    put(ing_ref, ing_out.at[0])
    for j in range(2):
        rows = pl.ds(j * 256, 256)
        for k in range(2):
            dbuf[rows, k * F:(k + 1) * F] = od_ref[2 * j + k].astype(f32)
        put(dbuf.at[rows], gdown_out.at[rows])
    for q in range(4):
        rows = pl.ds(q * 256, 256)
        ubuf[rows, :] = ou_ref[q].astype(f32)
        put(ubuf.at[rows], gup_out.at[rows])
    for i in range(3):
        qbuf[i] = ow_ref[i].astype(f32)
        put(qbuf.at[i], gq_out.at[i])
    for j in range(8):
        nbuf[:, j * C:(j + 1) * C] = ow_ref[3, j * C:(j + 1) * C, :].astype(f32)
    put(nbuf, gdn_out)
    gub_out[...] = sm_ref[5:6, 0:F]
    for i in range(3):
        gqb_out[i:i + 1, :] = sm_ref[5:6, F + i * C:F + (i + 1) * C]
    for i, ref in enumerate((ob_out, g1_out, b1_out, g2_out, b2_out)):
        ref[...] = sm_ref[i:i + 1, :]
    for cp in copies:
        cp.wait()


def widen(*args):
    vm = pl.BlockSpec(memory_space=pltpu.VMEM)
    hbm = pl.BlockSpec(memory_space=pl.ANY)
    one = jax.ShapeDtypeStruct((1, D), f32)
    return pl.pallas_call(
        widen_body,
        out_shape=[
            jax.ShapeDtypeStruct((1, 128, D), bf16),
            jax.ShapeDtypeStruct((1, 128, D), f32),
            jax.ShapeDtypeStruct((3, D, C), f32),
            jax.ShapeDtypeStruct((3, C), f32),
            jax.ShapeDtypeStruct((C, D), f32),
            jax.ShapeDtypeStruct((D, F), f32),
            jax.ShapeDtypeStruct((1, F), f32),
            jax.ShapeDtypeStruct((F, D), f32),
            one, one, one, one, one,
        ],
        in_specs=[hbm, hbm, vm, vm, vm, vm],
        out_specs=[hbm, hbm, hbm, vm, hbm, hbm, vm, hbm] + [vm] * 5,
        scratch_shapes=[
            pltpu.VMEM((F, D), f32), pltpu.VMEM((D, F), f32), pltpu.VMEM((3, D, C), f32), pltpu.VMEM((C, D), f32),
            pltpu.SemaphoreType.DMA((12,)),
        ],
        compiler_params=pltpu.CompilerParams(vmem_limit_bytes=63 * 1024 * 1024),
    )(*args)


def local(
    hidden_in, first_gain, first_shift, second_gain, second_shift, qkv_weight, qkv_bias, dense_weight,
    up_weight, up_bias, down_weight, out_bias, segments, positions, cotangent,
):
    parts = layer(
        hidden_in, cotangent, segments, positions, first_gain, first_shift, second_gain, second_shift, out_bias,
        up_bias, qkv_bias, qkv_weight, dense_weight, up_weight, down_weight,
    )
    act, ing, gq, gqb, gdn, gup, gub, gdown, ob, g1, b1, g2, b2 = widen(*parts)
    flat = lambda a: a.reshape(-1)
    return (act, ing, gq, gqb, gdn, gup, flat(gub), gdown, flat(ob), flat(g1), flat(b1), flat(g2), flat(b2))


def solution(mesh):
    placed = (
        P("dp", "tensor", None), P(), P(), P(), P(), P(None, None, "tensor"), P(None, "tensor"),
        P("tensor", None), P(None, "tensor"), P("tensor"), P("tensor", None), P(), P("dp", None),
        P("dp", None), P("dp", "tensor", None),
    )
    return jax.shard_map(
        local,
        mesh=mesh,
        in_specs=placed,
        out_specs=(
            P("dp", "tensor", None), P("dp", "tensor", None), P(None, None, "tensor"), P(None, "tensor"),
            P("tensor", None), P(None, "tensor"), P("tensor"), P("tensor", None), P(), P(), P(), P(), P(),
        ),
        check_vma=False,
    )
```

time: 134 us -> 118 us (0.88)
  local copies, waits for them, and re-layouts: 14.6 us -> 0 us
  other arithmetic: 9.01 us -> 0 us
  Pallas kernels: 109 us -> 116 us
    pallas_call x0 -> x1, Pallas kernels: none -> 27.5 us  [widen(): pl.pallas_call(widen_body, out_shape=[jax.ShapeDtypeStruct((1, 128, D), b...]
    pallas_call x1, Pallas kernels: 109 us -> 88.6 us  [layer(): pl.pallas_call(kernel_body, out_shape=[jax.ShapeDtypeStruct((128, D), bf1...]
    convert_element_type x2 -> x0, local copies, waits for them, and re-layouts: 6.09 us -> none  [local(): of[2:4].reshape(2, 256, 2, F).transpose(0, 2, 1, 3).reshape(D, F)]
    slice x4 -> x0, local copies, waits for them, and re-layouts: 4.17 us -> none  [the longest x1 1.56 us: local(): sm[4]]
    convert_element_type x4 -> x0, other arithmetic: 3.73 us -> none  [the longest x1 1.63 us: local(): grad_down = of[0:2].reshape(F, D).astype(f32)]
    another operation x5 -> x0, other arithmetic: 3.42 us -> none  [local(): jnp.stack([r.astype(f32) for r in rows] + [biases, consts, jnp.zeros((D,)...]
    unnamed x9 -> x0, local copies, waits for them, and re-layouts: 2.19 us -> none
    slice x1 -> x0, other arithmetic: 1.85 us -> none  [local(): grad_down = of[0:2].reshape(F, D).astype(f32)]
where the time goes in v2:
time: 118 us; the launch traced here: 117 us
  Pallas kernels  116 us (98%)
    pallas_call x1, Pallas kernels, layer(): pl.pallas_call(kernel_body, out_shape=[jax.ShapeDtypeStruct((128, D), bf1...  88.6 us
    pallas_call x1, Pallas kernels, widen(): pl.pallas_call(widen_body, out_shape=[jax.ShapeDtypeStruct((1, 128, D), b...  27.5 us

profile of v2, /device:TPU:0, one launch (start us, length us, event | category | flops | bytes accessed | tf_op | source)
XLA Modules:
  0.0 117.0 jit_solution(10545676455020478419)
XLA Ops:
  0.7 88.6 %shard_map.246 = (bf16[128,1024]{1,0:T(8,128)(2,1)}, f32[128,1024]{1,0:T(8,128)}, bf16[4,256,512]{2,1,0:T(8,128)(2,1)}, bf16[4,256,512]{2,1,0:T(8,128)(2,1)}, bf...) custom-call(bf16[1,128,1024]{2,1,0:T(8,128)(2,1)} %hid_ref.1, bf16[1,128,1024]{2,1,0:T(8,128)(2,1)} %cot_ref.1, ...), custom_call_target="tpu_custom_call" | custom-call | tf_op jit(solution)/shard_map/pallas_call | solution.py:606
  89.3 27.5 %shard_map.247 = (bf16[1,128,1024]{2,1,0:T(8,128)(2,1)}, f32[1,128,1024]{2,1,0:T(8,128)}, f32[3,1024,128]{2,1,0:T(8,128)}, f32[3,128]{1,0:T(4,128)}, f32[128,102...) custom-call(bf16[128,1024]{1,0:T(8,128)(2,1)} %get-tuple-element.32., ...), custom_call_target="tpu_custom_call" | custom-call | tf_op jit(solution)/shard_map/pallas_call | solution.py:667

commit v3 on v2

--- a/solution.py
+++ b/solution.py
@@ -40,7 +40,7 @@
     wqkv_ref, wd_ref, wup_ref, wdn_ref,
     act_out, ing_out, od_out, ou_out, ow_out, sm_out,
     hidf, cotf, xh, n1, n2, act_s, gel, gg, qs, ks, vs, ga, vT, kT, attT, att, gp,
-    dk, dv, wqkv, wd, wup, wdn, wcat, wcatT, wupT, wdnT, wdT, ct, st, segc, po, dxh,
+    dk, dv, dqT, wqkv, wd, wup, wdn, wcat, wcatT, wupT, wdnT, wdT, ct, st, segc, po, dxh,
     gd, rd_, od, gu, ru_, ou, gw, rw1, pw, rw2, ow,
     sa, ra, ssa, r1a, r2a, sd, rd, ssd, r1d, r2d, sm, smy, smz, smt,
     ssem, rsem, lsem,
@@ -336,54 +336,48 @@
     dk[...] = jnp.zeros_like(dk)
     dv[...] = jnp.zeros_like(dv)
 
-    def attention_block(i):
+    def attention_half(i, h):
         q0, L = i * 256, (i + 1) * 256
-        qb, gb = qs[q0:L, :], ga[q0:L, :]
         zero = jnp.zeros((), bf16)
         kidx = lax.broadcasted_iota(jnp.int32, (L, 256), 0)
         qidx = lax.broadcasted_iota(jnp.int32, (L, 256), 1) + q0
         sc = segc[0:L, :]
         same = jnp.concatenate([sc, sc], axis=1) == seg_ref[0:1, q0:L].astype(f32)
         allowed = same & (kidx <= qidx)
-        pbs, dss, qms, gms, outs, dqs = [], [], [], [], [], []
-        for h in range(2):
-            mine = (lane // HD) == h
-            qm, gm = jnp.where(mine, qb, zero), jnp.where(mine, gb, zero)
-            s = jnp.where(allowed, dot_nt(ks[0:L, :], qm), -1e30)
-            e = jnp.exp(s - jnp.max(s, axis=0, keepdims=True))
-            p = e * (1.0 / jnp.sum(e, axis=0, keepdims=True))
-            pb = p.astype(bf16)
-            dp_ = dot_nt(vs[0:L, :], gm)
-            ds = (p * (dp_ - jnp.sum(p * dp_, axis=0, keepdims=True))).astype(bf16)
-            outs.append(dot(vT[h * HD:(h + 1) * HD, 0:L], pb))
-            dqs.append(dot(kT[h * HD:(h + 1) * HD, 0:L], ds))
-            pbs.append(pb)
-            dss.append(ds)
-            qms.append(qm)
-            gms.append(gm)
-        dv[0:L, :] += dot(jnp.concatenate(pbs, axis=1), jnp.concatenate(gms, axis=0))
-        dk[0:L, :] += dot(jnp.concatenate(dss, axis=1), jnp.concatenate(qms, axis=0))
-        oT = jnp.concatenate(outs, axis=0)
-        attT[:, q0:L] = oT.astype(bf16)
-        att[q0:L, :] = oT.T.astype(bf16)
-        cb, sb = ct[q0:L, :], st[q0:L, :]
-        dq = jnp.concatenate(dqs, axis=0).T
-        gp[q0:L, 0:C] = ((dq * cb - partner(dq) * sb) * 0.125).astype(bf16)
-        dkb = dk[q0:L, :]
-        gp[q0:L, C:2 * C] = (dkb * cb - partner(dkb) * sb).astype(bf16)
-        gp[q0:L, 2 * C:] = dv[q0:L, :].astype(bf16)
-        sm[5:6, F:F + 3 * C] += jnp.sum(gp[q0:L, :].astype(f32), axis=0, keepdims=True)
-
-    attention_block(3)
+        mine = (lane // HD) == h
+        qm, gm = jnp.where(mine, qs[q0:L, :], zero), jnp.where(mine, ga[q0:L, :], zero)
+        s = jnp.where(allowed, dot_nt(ks[0:L, :], qm), -1e30)
+        e = jnp.exp(s - jnp.max(s, axis=0, keepdims=True))
+        p = e * (1.0 / jnp.sum(e, axis=0, keepdims=True))
+        pb = p.astype(bf16)
+        dp_ = dot_nt(vs[0:L, :], gm)
+        ds = (p * (dp_ - jnp.sum(p * dp_, axis=0, keepdims=True))).astype(bf16)
+        hr = slice(h * HD, (h + 1) * HD)
+        attT[hr, q0:L] = dot(vT[hr, 0:L], pb).astype(bf16)
+        dqT[hr, :] = dot(kT[hr, 0:L], ds)
+        dv[0:L, :] += dot(pb, gm)
+        dk[0:L, :] += dot(ds, qm)
+        if h == 1:
+            att[q0:L, :] = attT[:, q0:L].T
+            cb, sb = ct[q0:L, :], st[q0:L, :]
+            dq = dqT[...].T
+            gp[q0:L, 0:C] = ((dq * cb - partner(dq) * sb) * 0.125).astype(bf16)
+            dkb = dk[q0:L, :]
+            gp[q0:L, C:2 * C] = (dkb * cb - partner(dkb) * sb).astype(bf16)
+            gp[q0:L, 2 * C:] = dv[q0:L, :].astype(bf16)
+            sm[5:6, F:F + 3 * C] += jnp.sum(gp[q0:L, :].astype(f32), axis=0, keepdims=True)
+
+    attention_half(3, 0)
+    attention_half(3, 1)
     ard.step(0)
+    attention_half(2, 0)
+    attention_half(2, 1)
     aru.step(0)
-    attention_block(2)
+    attention_half(1, 0)
     ard.step(1)
-    aru.step(1)
-    attention_block(1)
-    ard.step(2)
-    aru.step(2)
-    attention_block(0)
+    attention_half(1, 1)
+    attention_half(0, 0)
+    attention_half(0, 1)
 
     class RingReduce:
         def __init__(self):
@@ -435,21 +429,26 @@
 
     arw = RingReduce()
 
-    @pl.loop(0, 4)
-    def _(i):
-        r = pl.ds(pl.multiple_of(i * 256, 256), 256)
+    def attention_grads(i):
+        r = slice(i * 256, (i + 1) * 256)
         res = dot_tn(n1[:, r], gp[...]).astype(bf16)
         gw[0, r, :] = res[:, 0:C]
         gw[1, r, :] = res[:, C:2 * C]
         gw[2, r, :] = res[:, 2 * C:]
         dn = dot(attT[...], cotf[:, r]).astype(bf16)
-        gw[3, pl.ds(pl.multiple_of(i * 256, 256), 128), :] = dn[:, 0:C]
-        gw[3, pl.ds(pl.multiple_of(i * 256 + 128, 128), 128), :] = dn[:, C:]
-
+        gw[3, i * 256:i * 256 + 128, :] = dn[:, 0:C]
+        gw[3, i * 256 + 128:i * 256 + 256, :] = dn[:, C:]
+
+    attention_grads(0)
+    aru.step(1)
+    ard.step(2)
+    attention_grads(1)
+    attention_grads(2)
+    attention_grads(3)
     arw.start(0)
     arw.start(1)
+    aru.step(2)
     ard.step(3)
-    aru.step(3)
 
     class Scatter:
         def __init__(self, full, s0, r0, ss, r1, r2):
@@ -495,8 +494,6 @@
         r = pl.ds(i * 256, 256)
         po[r, :] = dot(act_s[r, :], wdn[...]) + dot(att[r, :], wd[...])
         rsa.give(i)
-    ard.back(3)
-    aru.back(3)
     for i in range(4):
         r = pl.ds(i * 256, 256)
         xhb = xh[r, :].astype(f32)
@@ -510,8 +507,7 @@
         dxh[r, :] += g2c * g2
         rsd.give(i)
         if i == 1:
-            ard.back(2)
-            aru.back(2)
+            rsa.fold()
 
     small = {}
 
@@ -531,30 +527,32 @@
     small_send("y", 4, sm[...], smy, y)
     arw.step1(0)
     arw.step1(1)
-    rsa.fold()
-    ard.back(1)
-    aru.back(1)
+    aru.step(3)
+    ard.back(3)
+    rsd.fold()
+    small_send("z", 4, small_sum("y", 4, smy), smz, z)
     arw.step2(0)
     arw.step2(1)
-    rsd.fold()
-    small_send("z", 4, small_sum("y", 4, smy), smz, z)
-    arw.step3(0)
-    arw.step3(1)
-    rsa.second()
-    rsd.second()
+    aru.back(3)
+    ard.back(2)
     tot_dp = small_sum("z", 4, smz)
     sm_out[5:6, :] = tot_dp[5:6]
     small_send("t", 8, tot_dp, smt, tn)
-    ard.back(0)
-    move(od, od_out)
-    aru.back(0)
-    move(ou, ou_out)
+    rsa.second()
+    arw.step3(0)
+    arw.step3(1)
+    aru.back(2)
+    ard.back(1)
+    rsd.second()
+    aru.back(1)
 
     out_b = row_of(ob_ref)
     for half in range(2):
         hr = pl.ds(half * 64, 64)
         hb = hidf[pl.ds(pl.multiple_of(own + half * 64, 64), 64), :].astype(f32)
         act_out[hr, :] = (hb + rsa.result(half) + out_b).astype(bf16)
+    ard.back(0)
+    move(od, od_out)
     for half in range(2):
         hr = pl.ds(half * 64, 64)
         fr = pl.ds(pl.multiple_of(own + half * 64, 64), 64)
@@ -564,6 +562,8 @@
         ing_out[hr, :] = cotf[fr, :].astype(f32) + back
     sm_out[0:5, :] = small_sum("t", 8, smt)[0:5]
     sm_out[6:8, :] = jnp.zeros((2, D), f32)
+    aru.back(0)
+    move(ou, ou_out)
     arw.finish(0)
     arw.finish(1)
     move(ow, ow_out)
@@ -582,7 +582,7 @@
         v((1024, C), bf16), v((1024, C), bf16), v((1024, C), bf16), v((1024, C), bf16),
         v((C, 1024), bf16), v((C, 1024), bf16), v((C, 1024), bf16), v((1024, C), bf16),
         v((1024, 3 * C), bf16),
-        v((1024, C), f32), v((1024, C), f32),
+        v((1024, C), f32), v((1024, C), f32), v((C, 256), f32),
         v((3, 1024, C), bf16), v((C, D), bf16), v((D, F), bf16), v((F, D), bf16),
         v((1024, 3 * C), bf16), v((3 * C, 1024), bf16), v((F, 1024), bf16), v((1024, F), bf16), v((1024, C), bf16),
         v((1024, C), f32), v((1024, C), f32), v((1024, C), f32),
@@ -625,7 +625,7 @@
 def widen_body(
     act_ref, ing_ref, od_ref, ou_ref, ow_ref, sm_ref,
     act_out, ing_out, gq_out, gqb_out, gdn_out, gup_out, gub_out, gdown_out, ob_out, g1_out, b1_out, g2_out, b2_out,
-    dbuf, ubuf, qbuf, nbuf, sem,
+    act_v, ing_v, od_v, ou_v, ow_v, dbuf, ubuf, qbuf, nbuf, sem,
 ):
     copies = []
 
@@ -633,30 +633,43 @@
         cp = pltpu.make_async_copy(src, dst, sem.at[len(copies)])
         cp.start()
         copies.append(cp)
-
-    put(act_ref, act_out.at[0])
-    put(ing_ref, ing_out.at[0])
+        return cp
+
+    downs = [put(od_ref.at[pl.ds(2 * j, 2)], od_v.at[pl.ds(2 * j, 2)]) for j in range(2)]
+    ups = [put(ou_ref.at[pl.ds(2 * j, 2)], ou_v.at[pl.ds(2 * j, 2)]) for j in range(2)]
+    ows = put(ow_ref, ow_v)
+    ings = put(ing_ref, ing_v)
+    acts = put(act_ref, act_v)
+    outs = []
     for j in range(2):
         rows = pl.ds(j * 256, 256)
+        downs[j].wait()
         for k in range(2):
-            dbuf[rows, k * F:(k + 1) * F] = od_ref[2 * j + k].astype(f32)
-        put(dbuf.at[rows], gdown_out.at[rows])
+            dbuf[rows, k * F:(k + 1) * F] = od_v[2 * j + k].astype(f32)
+        outs.append(put(dbuf.at[rows], gdown_out.at[rows]))
     for q in range(4):
         rows = pl.ds(q * 256, 256)
-        ubuf[rows, :] = ou_ref[q].astype(f32)
-        put(ubuf.at[rows], gup_out.at[rows])
+        if q % 2 == 0:
+            ups[q // 2].wait()
+        ubuf[rows, :] = ou_v[q].astype(f32)
+        outs.append(put(ubuf.at[rows], gup_out.at[rows]))
+    ows.wait()
     for i in range(3):
-        qbuf[i] = ow_ref[i].astype(f32)
-        put(qbuf.at[i], gq_out.at[i])
+        qbuf[i] = ow_v[i].astype(f32)
+        outs.append(put(qbuf.at[i], gq_out.at[i]))
     for j in range(8):
-        nbuf[:, j * C:(j + 1) * C] = ow_ref[3, j * C:(j + 1) * C, :].astype(f32)
-    put(nbuf, gdn_out)
+        nbuf[:, j * C:(j + 1) * C] = ow_v[3, j * C:(j + 1) * C, :].astype(f32)
+    outs.append(put(nbuf, gdn_out))
+    ings.wait()
+    outs.append(put(ing_v, ing_out.at[0]))
+    acts.wait()
+    outs.append(put(act_v, act_out.at[0]))
     gub_out[...] = sm_ref[5:6, 0:F]
     for i in range(3):
         gqb_out[i:i + 1, :] = sm_ref[5:6, F + i * C:F + (i + 1) * C]
     for i, ref in enumerate((ob_out, g1_out, b1_out, g2_out, b2_out)):
         ref[...] = sm_ref[i:i + 1, :]
-    for cp in copies:
+    for cp in outs:
         cp.wait()
 
 
@@ -677,11 +690,13 @@
             jax.ShapeDtypeStruct((F, D), f32),
             one, one, one, one, one,
         ],
-        in_specs=[hbm, hbm, vm, vm, vm, vm],
+        in_specs=[hbm] * 5 + [vm],
         out_specs=[hbm, hbm, hbm, vm, hbm, hbm, vm, hbm] + [vm] * 5,
         scratch_shapes=[
+            pltpu.VMEM((128, D), bf16), pltpu.VMEM((128, D), f32), pltpu.VMEM((4, 256, F), bf16),
+            pltpu.VMEM((4, 256, F), bf16), pltpu.VMEM((4, 1024, C), bf16),
             pltpu.VMEM((F, D), f32), pltpu.VMEM((D, F), f32), pltpu.VMEM((3, D, C), f32), pltpu.VMEM((C, D), f32),
-            pltpu.SemaphoreType.DMA((12,)),
+            pltpu.SemaphoreType.DMA((24,)),
         ],
         compiler_params=pltpu.CompilerParams(vmem_limit_bytes=63 * 1024 * 1024),
     )(*args)

time: 118 us -> 91.8 us (0.78)
  Pallas kernels: 116 us -> 90.7 us
    pallas_call x1, Pallas kernels: 27.5 us -> 5.57 us  [widen(): pl.pallas_call(widen_body, out_shape=[jax.ShapeDtypeStruct((1, 128, D), b...]
    pallas_call x1, Pallas kernels: 88.6 us -> 85.1 us  [layer(): pl.pallas_call(kernel_body, out_shape=[jax.ShapeDtypeStruct((128, D), bf1...]
where the time goes in v3:
time: 91.8 us; the launch traced here: 91.5 us
  Pallas kernels  90.7 us (99%)
    pallas_call x1, Pallas kernels, layer(): pl.pallas_call(kernel_body, out_shape=[jax.ShapeDtypeStruct((128, D), bf1...  85.1 us
    pallas_call x1, Pallas kernels, widen(): pl.pallas_call(widen_body, out_shape=[jax.ShapeDtypeStruct((1, 128, D), b...  5.57 us

profile of v3, /device:TPU:0, one launch (start us, length us, event | category | flops | bytes accessed | tf_op | source)
XLA Modules:
  0.0 91.5 jit_solution(2685378329696304684)
XLA Ops:
  0.7 85.1 %shard_map.246 = (bf16[128,1024]{1,0:T(8,128)(2,1)}, f32[128,1024]{1,0:T(8,128)}, bf16[4,256,512]{2,1,0:T(8,128)(2,1)}, bf16[4,256,512]{2,1,0:T(8,128)(2,1)}, bf...) custom-call(bf16[1,128,1024]{2,1,0:T(8,128)(2,1)} %hid_ref.1, bf16[1,128,1024]{2,1,0:T(8,128)(2,1)} %cot_ref.1, ...), custom_call_target="tpu_custom_call" | custom-call | tf_op jit(solution)/shard_map/pallas_call | solution.py:606
  85.8 5.6 %shard_map.247 = (bf16[1,128,1024]{2,1,0:T(8,128)(2,1)}, f32[1,128,1024]{2,1,0:T(8,128)}, f32[3,1024,128]{2,1,0:T(8,128)}, f32[3,128]{1,0:T(4,128)}, f32[128,102...) custom-call(bf16[128,1024]{1,0:T(8,128)(2,1)} %get-tuple-element.32., ...), custom_call_target="tpu_custom_call" | custom-call | tf_op jit(solution)/shard_map/pallas_call | solution.py:680

commit v4 on v3

--- a/solution.py
+++ b/solution.py
@@ -41,8 +41,8 @@
     act_out, ing_out, od_out, ou_out, ow_out, sm_out,
     hidf, cotf, xh, n1, n2, act_s, gel, gg, qs, ks, vs, ga, vT, kT, attT, att, gp,
     dk, dv, dqT, wqkv, wd, wup, wdn, wcat, wcatT, wupT, wdnT, wdT, ct, st, segc, po, dxh,
-    gd, rd_, od, gu, ru_, ou, gw, rw1, pw, rw2, ow,
-    sa, ra, ssa, r1a, r2a, sd, rd, ssd, r1d, r2d, sm, smy, smz, smt,
+    gd, rd_, od, gu, ru_, ou, gw, rw, ow,
+    sa, ra, ssa, r1a, r2a, sd, rd, ssd, r1d, r2d, sm, smy, smz, smt, act_v, ing_v, sm_v,
     ssem, rsem, lsem,
 ):
     dp = lax.axis_index("dp")
@@ -379,55 +379,7 @@
     attention_half(0, 0)
     attention_half(0, 1)
 
-    class RingReduce:
-        def __init__(self):
-            self.ax = (("y", y, "z", z), ("z", z, "y", y))
-            self.cp = {}
-
-        def start(self, a):
-            ax, me, _, _ = self.ax[a]
-            for k in (2, 1, 3):
-                to = pl.multiple_of((me + k) % 4 * 256, 256)
-                self.cp[a, 0, k] = send(gw.at[pl.ds(2 * a, 2), pl.ds(to, 256)], rw1.at[a, k - 1], (ax, k))
-
-        def step1(self, a):
-            _, me, ax, other = self.ax[a]
-            for k in (1, 3, 2):
-                self.cp[a, 0, k].wait_recv()
-            tot = gw[pl.ds(2 * a, 2), pl.ds(pl.multiple_of(me * 256, 256), 256), :].astype(f32)
-            for k in range(3):
-                tot = tot + rw1[a, k].astype(f32)
-            pw[a] = tot.astype(bf16)
-            for k in (2, 1, 3):
-                to = pl.multiple_of((other + k) % 4 * 64, 64)
-                self.cp[a, 1, k] = send(pw.at[a, :, pl.ds(to, 64)], rw2.at[a, k - 1], (ax, k))
-
-        def step2(self, a):
-            _, me, ax, other = self.ax[a]
-            for k in (1, 3, 2):
-                self.cp[a, 1, k].wait_recv()
-            tot = pw[a, :, pl.ds(pl.multiple_of(other * 64, 64), 64), :].astype(f32)
-            for k in range(3):
-                tot = tot + rw2[a, k].astype(f32)
-            mine = pl.ds(pl.multiple_of(me * 256 + other * 64, 64), 64)
-            ow[pl.ds(2 * a, 2), mine, :] = tot.astype(bf16)
-            ref = ow.at[pl.ds(2 * a, 2), mine]
-            for k in (2, 1, 3):
-                self.cp[a, 2, k] = send(ref, ref, (ax, k))
-
-        def step3(self, a):
-            ax, me, _, _ = self.ax[a]
-            for k in (1, 3, 2):
-                self.cp[a, 2, k].wait_recv()
-            ref = ow.at[pl.ds(2 * a, 2), pl.ds(pl.multiple_of(me * 256, 256), 256)]
-            for k in (2, 1, 3):
-                self.cp[a, 3, k] = send(ref, ref, (ax, k))
-
-        def finish(self, a):
-            for k in (1, 3, 2):
-                self.cp[a, 3, k].wait_recv()
-
-    arw = RingReduce()
+    arw = AllReduce(gw, rw, ow, 1024)
 
     def attention_grads(i):
         r = slice(i * 256, (i + 1) * 256)
@@ -446,7 +398,6 @@
     attention_grads(2)
     attention_grads(3)
     arw.start(0)
-    arw.start(1)
     aru.step(2)
     ard.step(3)
 
@@ -507,6 +458,9 @@
         dxh[r, :] += g2c * g2
         rsd.give(i)
         if i == 1:
+            arw.step(0)
+            aru.step(3)
+            ard.back(3)
             rsa.fold()
 
     small = {}
@@ -525,32 +479,34 @@
         return tot
 
     small_send("y", 4, sm[...], smy, y)
-    arw.step1(0)
-    arw.step1(1)
-    aru.step(3)
-    ard.back(3)
+    arw.step(1)
+    aru.back(3)
+    ard.back(2)
     rsd.fold()
     small_send("z", 4, small_sum("y", 4, smy), smz, z)
-    arw.step2(0)
-    arw.step2(1)
-    aru.back(3)
-    ard.back(2)
+    arw.step(2)
+    aru.back(2)
+    rsa.second()
+    arw.step(3)
+    ard.back(1)
     tot_dp = small_sum("z", 4, smz)
-    sm_out[5:6, :] = tot_dp[5:6]
+    sm_v[5:6, :] = tot_dp[5:6]
     small_send("t", 8, tot_dp, smt, tn)
-    rsa.second()
-    arw.step3(0)
-    arw.step3(1)
-    aru.back(2)
-    ard.back(1)
+    arw.back(3)
+    aru.back(1)
+    sent = len(pending)
+    arw.back(2)
     rsd.second()
-    aru.back(1)
+    arw.back(1)
+    for cp in pending[:sent]:
+        cp.wait_send()
 
     out_b = row_of(ob_ref)
     for half in range(2):
         hr = pl.ds(half * 64, 64)
         hb = hidf[pl.ds(pl.multiple_of(own + half * 64, 64), 64), :].astype(f32)
-        act_out[hr, :] = (hb + rsa.result(half) + out_b).astype(bf16)
+        act_v[hr, :] = (hb + rsa.result(half) + out_b).astype(bf16)
+    move(act_v, act_out)
     ard.back(0)
     move(od, od_out)
     for half in range(2):
@@ -559,17 +515,18 @@
         d = rsd.result(half)
         xhat, rstd = norm_stats(hidf[fr, :].astype(f32))
         back = (d - jnp.mean(d, axis=1, keepdims=True) - xhat * jnp.mean(d * xhat, axis=1, keepdims=True)) * rstd
-        ing_out[hr, :] = cotf[fr, :].astype(f32) + back
-    sm_out[0:5, :] = small_sum("t", 8, smt)[0:5]
-    sm_out[6:8, :] = jnp.zeros((2, D), f32)
+        ing_v[hr, :] = cotf[fr, :].astype(f32) + back
+    move(ing_v, ing_out)
+    sm_v[0:5, :] = small_sum("t", 8, smt)[0:5]
+    sm_v[6:8, :] = jnp.zeros((2, D), f32)
+    move(sm_v, sm_out)
     aru.back(0)
     move(ou, ou_out)
-    arw.finish(0)
-    arw.finish(1)
+    arw.back(0)
     move(ow, ow_out)
-    for cp in pending:
+    for cp in pending[sent:]:
         cp.wait_send()
-    for cp in moves[-3:]:
+    for cp in moves[-6:]:
         cp.wait()
 
 
@@ -591,8 +548,7 @@
     for _ in range(2):
         scratch += [v((4, 256, F), bf16), v((4, 256, F), bf16), v((4, 256, F), bf16)]
     scratch += [
-        v((4, 1024, C), bf16), v((2, 3, 2, 256, C), bf16), v((2, 2, 256, C), bf16), v((2, 3, 2, 64, C), bf16),
-        v((4, 1024, C), bf16),
+        v((4, 1024, C), bf16), v((4, 1024, C), bf16), v((4, 1024, C), bf16),
     ]
     for _ in range(2):
         scratch += [
@@ -600,6 +556,7 @@
             v((2, 64, D), bf16),
         ]
     scratch += [v((8, D), f32), v((4, 8, D), f32), v((4, 8, D), f32), v((8, 8, D), f32)]
+    scratch += [v((128, D), bf16), v((128, D), f32), v((8, D), f32)]
     scratch += [pltpu.SemaphoreType.DMA((NSEM,)), pltpu.SemaphoreType.DMA((NSEM,)), pltpu.SemaphoreType.DMA((12,))]
     vm = pl.BlockSpec(memory_space=pltpu.VMEM)
     hbm = pl.BlockSpec(memory_space=pl.ANY)
@@ -614,7 +571,7 @@
             jax.ShapeDtypeStruct((8, D), f32),
         ],
         in_specs=[hbm, hbm] + [vm] * 9 + [hbm] * 4,
-        out_specs=[vm, vm, hbm, hbm, hbm, vm],
+        out_specs=[hbm] * 6,
         scratch_shapes=scratch,
         compiler_params=pltpu.CompilerParams(
             collective_id=0, has_side_effects=True, vmem_limit_bytes=63 * 1024 * 1024
@@ -625,7 +582,7 @@
 def widen_body(
     act_ref, ing_ref, od_ref, ou_ref, ow_ref, sm_ref,
     act_out, ing_out, gq_out, gqb_out, gdn_out, gup_out, gub_out, gdown_out, ob_out, g1_out, b1_out, g2_out, b2_out,
-    act_v, ing_v, od_v, ou_v, ow_v, dbuf, ubuf, qbuf, nbuf, sem,
+    act_v, ing_v, od_v, ou_v, ow_v, sm_v, dbuf, ubuf, qbuf, nbuf, rowb, upb, qkvb, sem,
 ):
     copies = []
 
@@ -640,6 +597,7 @@
     ows = put(ow_ref, ow_v)
     ings = put(ing_ref, ing_v)
     acts = put(act_ref, act_v)
+    sms = put(sm_ref, sm_v)
     outs = []
     for j in range(2):
         rows = pl.ds(j * 256, 256)
@@ -664,17 +622,20 @@
     outs.append(put(ing_v, ing_out.at[0]))
     acts.wait()
     outs.append(put(act_v, act_out.at[0]))
-    gub_out[...] = sm_ref[5:6, 0:F]
+    sms.wait()
+    upb[...] = sm_v[5:6, 0:F]
+    outs.append(put(upb, gub_out))
     for i in range(3):
-        gqb_out[i:i + 1, :] = sm_ref[5:6, F + i * C:F + (i + 1) * C]
+        qkvb[i:i + 1, :] = sm_v[5:6, F + i * C:F + (i + 1) * C]
+    outs.append(put(qkvb, gqb_out))
     for i, ref in enumerate((ob_out, g1_out, b1_out, g2_out, b2_out)):
-        ref[...] = sm_ref[i:i + 1, :]
+        rowb[i] = sm_v[i:i + 1, :]
+        outs.append(put(rowb.at[i], ref))
     for cp in outs:
         cp.wait()
 
 
 def widen(*args):
-    vm = pl.BlockSpec(memory_space=pltpu.VMEM)
     hbm = pl.BlockSpec(memory_space=pl.ANY)
     one = jax.ShapeDtypeStruct((1, D), f32)
     return pl.pallas_call(
@@ -690,13 +651,15 @@
             jax.ShapeDtypeStruct((F, D), f32),
             one, one, one, one, one,
         ],
-        in_specs=[hbm] * 5 + [vm],
-        out_specs=[hbm, hbm, hbm, vm, hbm, hbm, vm, hbm] + [vm] * 5,
+        in_specs=[hbm] * 6,
+        out_specs=[hbm] * 13,
         scratch_shapes=[
             pltpu.VMEM((128, D), bf16), pltpu.VMEM((128, D), f32), pltpu.VMEM((4, 256, F), bf16),
             pltpu.VMEM((4, 256, F), bf16), pltpu.VMEM((4, 1024, C), bf16),
+            pltpu.VMEM((8, D), f32),
             pltpu.VMEM((F, D), f32), pltpu.VMEM((D, F), f32), pltpu.VMEM((3, D, C), f32), pltpu.VMEM((C, D), f32),
-            pltpu.SemaphoreType.DMA((24,)),
+            pltpu.VMEM((5, 1, D), f32), pltpu.VMEM((1, F), f32), pltpu.VMEM((3, C), f32),
+            pltpu.SemaphoreType.DMA((32,)),
         ],
         compiler_params=pltpu.CompilerParams(vmem_limit_bytes=63 * 1024 * 1024),
     )(*args)

time: 91.8 us -> 89.5 us (0.975)
  Pallas kernels: 90.7 us -> 88.5 us
    pallas_call x1, Pallas kernels: 5.57 us -> 4.28 us  [widen(): pl.pallas_call(widen_body, out_shape=[jax.ShapeDtypeStruct((1, 128, D), b...]
where the time goes in v4:
time: 89.5 us; the launch traced here: 89.3 us
  Pallas kernels  88.5 us (99%)
    pallas_call x1, Pallas kernels, layer(): pl.pallas_call(kernel_body, out_shape=[jax.ShapeDtypeStruct((128, D), bf1...  84.2 us
    pallas_call x1, Pallas kernels, widen(): pl.pallas_call(widen_body, out_shape=[jax.ShapeDtypeStruct((1, 128, D), b...  4.28 us

profile of v4, /device:TPU:0, one launch (start us, length us, event | category | flops | bytes accessed | tf_op | source)
XLA Modules:
  0.0 89.3 jit_solution(4041544627957457665)
XLA Ops:
  0.7 84.2 %shard_map.246 = (bf16[128,1024]{1,0:T(8,128)(2,1)}, f32[128,1024]{1,0:T(8,128)}, bf16[4,256,512]{2,1,0:T(8,128)(2,1)}, bf16[4,256,512]{2,1,0:T(8,128)(2,1)}, bf...) custom-call(bf16[1,128,1024]{2,1,0:T(8,128)(2,1)} %hid_ref.1, bf16[1,128,1024]{2,1,0:T(8,128)(2,1)} %cot_ref.1, ...), custom_call_target="tpu_custom_call" | custom-call | tf_op jit(solution)/shard_map/pallas_call | solution.py:563
  84.9 4.3 %shard_map.247 = (bf16[1,128,1024]{2,1,0:T(8,128)(2,1)}, f32[1,128,1024]{2,1,0:T(8,128)}, f32[3,1024,128]{2,1,0:T(8,128)}, f32[3,128]{1,0:T(4,128)}, f32[128,102...) custom-call(bf16[128,1024]{1,0:T(8,128)(2,1)} %get-tuple-element.32., ...), custom_call_target="tpu_custom_call" | custom-call | tf_op jit(solution)/shard_map/pallas_call | solution.py:641
